TPU v7x, 32 devices: a whole 2x2x4 slice. The times are simulated.
32 devices in a mesh: ctx: 16 (over z, x, core), head: 2 (over y).
Axes of the slice: x: 2, y: 2, z: 4, core: 2. Of those that a mesh axis runs over, the one named last changes fastest.
Arguments:
- queries: bfloat16 [8192, 16, 128], P('ctx', 'head'), may hold values from -40 to 40
- keys: bfloat16 [8192, 128], P('ctx'), may hold values from -5 to 5
- values: bfloat16 [8192, 128], P('ctx'), may hold values from -1.5 to 1.5
- grad_out: bfloat16 [8192, 16, 128], P('ctx', 'head'), may hold values from -6 to 6
- lengths: int32 [16], replicated, may hold values from 1 to 1024, 8192 in all
- tile_of: int32 [16], replicated, may hold values from 0 to 15, each once
Outputs:
- attended: bfloat16 [8192, 16, 128], P('ctx', 'head')
- grad_queries: bfloat16 [8192, 16, 128], P('ctx', 'head')
- grad_keys: float32 [8192, 128], P('ctx')
- grad_values: float32 [8192, 128], P('ctx')
Inputs may be any that keep to these rules, and one draw needn't show every extreme that they name: 16 positive lengths summing to 8192; the longest is exactly 1024. `tile_of`: each tile number appears once.
All inputs are finite; a program needn't handle non-finite values.
Results may differ from a plain program's by a relative error of at most 0.025.
Values may be sent and summed in bfloat16 or wider, within the bound.
No kernel may reach another device: no remote copies, remote signals or barrier semaphores. Data moves between devices by JAX's collectives and lax.ppermute only.
A program may use at most 128 MiB of HBM per device.

v0:
```python
import functools

import jax
import jax.numpy as jnp
from jax import lax
from jax.experimental import pallas as pl
from jax.experimental.pallas import tpu as pltpu
from jax.sharding import PartitionSpec as P

LOG2E = 1.4426950408889634
NEG_FILL = -1e30
KEY_BLOCK = 256
ROW_BLOCK = 1024
VMEM_LIMIT = 60 * 1024 * 1024
SMALL_LIMIT = 16 * 1024 * 1024
SMEM = pl.BlockSpec(memory_space=pltpu.SMEM)
VMEM = pl.BlockSpec(memory_space=pltpu.VMEM)
HBM = pl.BlockSpec(memory_space=pl.ANY)
F32 = jnp.float32
BF16 = jnp.bfloat16


def matmul(left, right):
    return lax.dot_general(left, right, (((1,), (0,)), ((), ())), preferred_element_type=F32)


def matmul_first(left, right):
    return lax.dot_general(left, right, (((0,), (0,)), ((), ())), preferred_element_type=F32)


def matmul_last(left, right):
    return lax.dot_general(left, right, (((1,), (1,)), ((), ())), preferred_element_type=F32)


def fold_rows(block, combine):
    folded = block[0:8]
    for begin in range(8, block.shape[0], 8):
        folded = combine(folded, block[begin : begin + 8])
    return folded


def document_starts(ends, positions):
    start = jnp.zeros_like(positions)
    for end in ends:
        start = jnp.where(end <= positions, end, start)
    return start


def document_ends(lengths_ref):
    ends = []
    total = jnp.int32(0)
    for doc in range(lengths_ref.shape[0]):
        total = total + lengths_ref[doc]
        ends.append(total)
    return ends


def lane_positions(heads, first_pos):
    lane = lax.broadcasted_iota(jnp.int32, (1, ROW_BLOCK), 1)
    return first_pos + lax.div(lane, heads)


def key_positions(keys):
    shape = (keys.stop - keys.start, ROW_BLOCK)
    return keys.start + lax.broadcasted_iota(jnp.int32, shape, 0)


def fold_all(blocks, combine):
    folded = fold_rows(blocks[0], combine)
    for block in blocks[1:]:
        folded = combine(folded, fold_rows(block, combine))
    return folded


def row_blocks(total):
    return [slice(begin, begin + ROW_BLOCK) for begin in range(0, total, ROW_BLOCK)]


def key_blocks(begin, end):
    starts = list(range(end - KEY_BLOCK, begin, -KEY_BLOCK))[::-1]
    starts = [begin] + [start for start in starts if start > begin]
    return [slice(start, stop) for start, stop in zip(starts, starts[1:] + [end])]


def own_forward_kernel(
    heads, place_ref, lengths_ref, tile_of_ref, q_ref, g_ref, k_ref, v_ref, stats_ref, *weight_refs
):
    tile_rows, width = k_ref.shape
    exponent_scale = float(width) ** (-0.5) * LOG2E
    chunk_pos = ROW_BLOCK // heads
    tile_begin = tile_of_ref[place_ref[0]] * tile_rows
    ends = document_ends(lengths_ref)

    for chunk, rows in enumerate(row_blocks(q_ref.shape[0])):
        first_pos = tile_begin + chunk * chunk_pos
        q_pos = lane_positions(heads, first_pos)
        low = document_starts(ends, q_pos) - tile_begin
        high = q_pos - tile_begin
        blocks = key_blocks(0, (chunk + 1) * chunk_pos)
        scores = []
        for keys in blocks:
            score = matmul_last(k_ref[keys, :], q_ref[rows, :])
            key_pos = key_positions(keys)
            live = key_pos >= low
            if keys.stop > chunk * chunk_pos:
                live = live & (key_pos <= high)
            scores.append(jnp.where(live, score, NEG_FILL))
        top = jnp.max(fold_all(scores, jnp.maximum), axis=0, keepdims=True) * exponent_scale
        sums = jnp.zeros((8, ROW_BLOCK), F32)
        products = jnp.zeros((8, ROW_BLOCK), F32)
        for keys, score in zip(blocks, scores):
            weight = jnp.exp2(score * exponent_scale - top)
            weight_refs[chunk][keys, :] = weight.astype(BF16)
            dprob = matmul_last(v_ref[keys, :], g_ref[rows, :])
            sums += fold_rows(weight, jnp.add)
            products += fold_rows(weight * dprob, jnp.add)
        stats_ref[0:1, rows] = top
        stats_ref[1:2, rows] = jnp.sum(sums, axis=0, keepdims=True)
        stats_ref[2:3, rows] = jnp.sum(products, axis=0, keepdims=True)


class Past:
    def __init__(self, window, heads, place_ref, lengths_ref, tile_of_ref, past_hbm, win_ref):
        n_owners, _, _, self.piece, self.width = past_hbm.shape
        self.n_owners = n_owners
        self.tile_rows = n_owners * self.piece
        self.past_rows = window * self.tile_rows
        self.chunk_pos = ROW_BLOCK // heads
        self.heads = heads
        self.window = window
        self.past_hbm = past_hbm
        self.win_ref = win_ref
        self.tile_begin = tile_of_ref[place_ref[0]] * self.tile_rows
        first_start, self.first_end = jnp.int32(0), jnp.int32(0)
        for end in document_ends(lengths_ref):
            crosses = (self.first_end <= self.tile_begin) & (end > self.tile_begin)
            first_start = jnp.where(end <= self.tile_begin, end, first_start)
            self.first_end = jnp.where(crosses, end, self.first_end)
        self.first_key = jnp.maximum(self.past_rows - (self.tile_begin - first_start), 0)
        self.unit = window * KEY_BLOCK // 4
        self.branches = self.past_rows // self.unit
        self.all_units = self.branches - lax.div(self.first_key, self.unit)

    def copies(self, part, sem):
        return [
            pltpu.make_async_copy(
                self.past_hbm.at[:, slot, part],
                self.win_ref.at[part, slot],
                sem.at[part, slot],
            )
            for slot in range(self.window)
        ]

    def rows(self, part, keys):
        slot, begin = divmod(keys.start, self.tile_rows)
        end = begin + keys.stop - keys.start
        if end > self.tile_rows:
            border = (slot + 1) * self.tile_rows
            parts = [
                self.rows(part, slice(keys.start, border)),
                self.rows(part, slice(border, keys.stop)),
            ]
            return jnp.concatenate(parts, axis=0)
        if self.n_owners == 1:
            return self.win_ref[part, slot, 0, begin:end, :]
        rows = self.win_ref[part, slot, begin // self.piece : end // self.piece]
        return rows.reshape(end - begin, self.width)

    def scores(self, units, q_rows):
        blocks = key_blocks(self.past_rows - units * self.unit, self.past_rows)
        scores = [matmul_last(self.rows(0, keys), q_rows) for keys in blocks]
        live = key_positions(blocks[0]) >= self.first_key
        scores[0] = jnp.where(live, scores[0], NEG_FILL)
        return blocks, scores

    def by_units(self, chunk, nothing, branch):
        first_pos = self.tile_begin + chunk * self.chunk_pos
        live_units = jnp.where(first_pos < self.first_end, self.all_units, 0)
        pl.when(live_units == 0)(nothing)
        for units in range(1, self.branches + 1):
            pl.when(live_units == units)(functools.partial(branch, units))

    def has_past(self, chunk):
        first_pos = self.tile_begin + chunk * self.chunk_pos
        return lane_positions(self.heads, first_pos) < self.first_end


def chunk_rows(chunk):
    return pl.ds(pl.multiple_of(chunk * ROW_BLOCK, ROW_BLOCK), ROW_BLOCK)


def chunk_copies(pairs, sem, chunk):
    rows = chunk_rows(chunk)
    copies = []
    for index, (source, target, axis) in enumerate(pairs):
        where = (rows, slice(None)) if axis == 0 else (slice(None), rows)
        copies.append(
            pltpu.make_async_copy(source.at[where], target.at[where], sem.at[chunk, index])
        )
    return copies


def start_all(copies):
    for copy in copies:
        copy.start()


def wait_all(copies):
    for copy in copies:
        copy.wait()


def past_kernel(
    window,
    heads,
    place_ref,
    lengths_ref,
    tile_of_ref,
    q_hbm,
    g_hbm,
    own_stats_hbm,
    past_hbm,
    stats_hbm,
    terms_hbm,
    q_ref,
    g_ref,
    own_stats_ref,
    stats_ref,
    win_ref,
    terms_ref,
    dk_acc,
    dv_acc,
    in_sem,
    past_sem,
    stats_sem,
    terms_sem,
):
    past = Past(window, heads, place_ref, lengths_ref, tile_of_ref, past_hbm, win_ref)
    past_rows, width = dk_acc.shape
    scale = float(width) ** (-0.5)
    exponent_scale = scale * LOG2E
    chunks = q_ref.shape[0] // ROW_BLOCK
    pairs = ((q_hbm, q_ref, 0), (g_hbm, g_ref, 0))
    stats_in = pltpu.make_async_copy(own_stats_hbm, own_stats_ref, stats_sem.at[0])
    stats_out = pltpu.make_async_copy(stats_ref, stats_hbm, stats_sem.at[1])

    start_all(past.copies(0, past_sem))
    start_all(chunk_copies(pairs, in_sem, 0))
    stats_in.start()
    start_all(past.copies(1, past_sem))
    for chunk in range(1, chunks):
        start_all(chunk_copies(pairs, in_sem, chunk))
    dk_acc[...] = jnp.zeros_like(dk_acc)
    dv_acc[...] = jnp.zeros_like(dv_acc)
    wait_all(past.copies(0, past_sem) + past.copies(1, past_sem) + [stats_in])

    def chunk_step(chunk, carry):
        rows = chunk_rows(chunk)
        wait_all(chunk_copies(pairs, in_sem, chunk))
        own_top = own_stats_ref[0:1, rows]
        own_sum = own_stats_ref[1:2, rows]
        own_product = own_stats_ref[2:3, rows]

        def branch(units):
            has_past = past.has_past(chunk)
            q_rows = q_ref[rows, :]
            g_rows = g_ref[rows, :]
            blocks, scores = past.scores(units, q_rows)
            dprobs = [matmul_last(past.rows(1, keys), g_rows) for keys in blocks]
            top = jnp.max(fold_all(scores, jnp.maximum), axis=0, keepdims=True)
            top = jnp.where(has_past, jnp.maximum(top * exponent_scale, own_top), own_top)
            shift = jnp.where(has_past, top, -NEG_FILL)
            sums = jnp.zeros((8, ROW_BLOCK), F32)
            products = jnp.zeros((8, ROW_BLOCK), F32)
            weights = []
            for score, dprob in zip(scores, dprobs):
                weight = jnp.exp2(score * exponent_scale - shift)
                sums += fold_rows(weight, jnp.add)
                products += fold_rows(weight * dprob, jnp.add)
                weights.append(weight.astype(BF16))
            rescale = jnp.exp2(own_top - top)
            total = own_sum * rescale + jnp.sum(sums, axis=0, keepdims=True)
            product = own_product * rescale + jnp.sum(products, axis=0, keepdims=True)
            inverse = 1.0 / total
            delta = product * inverse
            stats_ref[0:1, rows] = rescale * inverse
            stats_ref[1:2, rows] = delta
            stats_ref[2:3, rows] = jnp.where(has_past, top + jnp.log2(total), -NEG_FILL)
            inverse_low = inverse.astype(BF16)
            probs = [weight * inverse_low for weight in weights]
            for keys, prob in zip(blocks, probs):
                dv_acc[keys, :] += matmul(prob, g_rows)
            for keys, prob, dprob in zip(blocks, probs, dprobs):
                dscore = prob * (dprob - delta).astype(BF16)
                dk_acc[keys, :] += matmul(dscore, q_rows)

        def nothing():
            inverse = 1.0 / own_sum
            stats_ref[0:1, rows] = inverse
            stats_ref[1:2, rows] = own_product * inverse
            stats_ref[2:3, rows] = jnp.full((1, ROW_BLOCK), -NEG_FILL, F32)

        past.by_units(chunk, nothing, branch)
        return carry

    lax.fori_loop(0, chunks, chunk_step, 0)
    stats_out.start()
    copies = [stats_out]
    for slot in range(window):
        rows = slice(slot * past.tile_rows, (slot + 1) * past.tile_rows)
        shape = (past.n_owners, past.piece, width)
        terms_ref[0, slot] = (dk_acc[rows, :] * scale).astype(BF16).reshape(shape)
        terms_ref[1, slot] = dv_acc[rows, :].astype(BF16).reshape(shape)
        for part in range(2):
            copy = pltpu.make_async_copy(
                terms_ref.at[part, slot], terms_hbm.at[:, slot, part], terms_sem.at[part, slot]
            )
            copy.start()
            copies.append(copy)
    wait_all(copies)


def late_kernel(
    window,
    heads,
    place_ref,
    lengths_ref,
    tile_of_ref,
    q_hbm,
    g_hbm,
    stats_hbm,
    past_hbm,
    own_out_hbm,
    own_dq_hbm,
    summed_hbm,
    att_hbm,
    dq_hbm,
    q_ref,
    g_ref,
    stats_ref,
    win_ref,
    own_out_ref,
    own_dq_ref,
    att_ref,
    dq_ref,
    in_sem,
    past_sem,
    stats_sem,
    out_sem,
):
    past = Past(window, heads, place_ref, lengths_ref, tile_of_ref, past_hbm, win_ref)
    width = past.width
    scale = float(width) ** (-0.5)
    exponent_scale = scale * LOG2E
    chunks = q_ref.shape[0] // ROW_BLOCK
    pairs = (
        (q_hbm, q_ref, 0),
        (g_hbm, g_ref, 0),
        (own_out_hbm, own_out_ref, 1),
        (own_dq_hbm, own_dq_ref, 1),
    )
    out_pairs = ((att_ref, att_hbm, 0), (dq_ref, dq_hbm, 0))
    stats_in = pltpu.make_async_copy(stats_hbm, stats_ref, stats_sem.at[0])
    start_all(past.copies(0, past_sem) + past.copies(1, past_sem) + [stats_in])
    for chunk in range(chunks):
        start_all(chunk_copies(pairs, in_sem, chunk))
    wait_all(past.copies(0, past_sem) + past.copies(1, past_sem) + [stats_in])

    def chunk_step(chunk, carry):
        rows = chunk_rows(chunk)
        wait_all(chunk_copies(pairs, in_sem, chunk))

        def branch(units):
            q_rows = q_ref[rows, :]
            g_rows = g_ref[rows, :]
            delta = stats_ref[1:2, rows]
            shift = stats_ref[2:3, rows]
            blocks, scores = past.scores(units, q_rows)
            out_turned = own_out_ref[:, rows].astype(F32)
            dq_turned = own_dq_ref[:, rows].astype(F32)
            for keys, score in zip(blocks, scores):
                prob = jnp.exp2(score * exponent_scale - shift).astype(BF16)
                out_turned += matmul_first(past.rows(1, keys), prob)
                dprob = matmul_last(past.rows(1, keys), g_rows)
                dscore = prob * (dprob - delta).astype(BF16)
                dq_turned += matmul_first(past.rows(0, keys), dscore)
            att_ref[rows, :] = out_turned.astype(BF16).T
            dq_ref[rows, :] = (dq_turned * scale).astype(BF16).T

        def nothing():
            att_ref[rows, :] = own_out_ref[:, rows].T
            dq_ref[rows, :] = (own_dq_ref[:, rows].astype(F32) * scale).astype(BF16).T

        past.by_units(chunk, nothing, branch)
        start_all(chunk_copies(out_pairs, out_sem, chunk))
        return carry

    lax.fori_loop(0, chunks, chunk_step, 0)
    for chunk in range(chunks):
        wait_all(chunk_copies(out_pairs, out_sem, chunk))


def own_grads_kernel(
    heads, q_ref, g_ref, stats_ref, k_ref, v_ref, *refs
):
    tile_rows, width = k_ref.shape
    chunk_pos = ROW_BLOCK // heads
    chunks = q_ref.shape[0] // ROW_BLOCK
    weight_refs = refs[:chunks]
    out_ref, dq_ref, dkv_ref, dk_acc, dv_acc = refs[chunks:]
    scale = float(width) ** (-0.5)
    dk_acc[...] = jnp.zeros_like(dk_acc)
    dv_acc[...] = jnp.zeros_like(dv_acc)

    for chunk, rows in enumerate(row_blocks(q_ref.shape[0])):
        rescale = stats_ref[0:1, rows]
        delta = stats_ref[1:2, rows]
        q_rows = q_ref[rows, :]
        g_rows = g_ref[rows, :]
        out_turned = jnp.zeros((width, ROW_BLOCK), F32)
        dq_turned = jnp.zeros((width, ROW_BLOCK), F32)
        for keys in key_blocks(0, (chunk + 1) * chunk_pos):
            prob = (weight_refs[chunk][keys, :].astype(F32) * rescale).astype(BF16)
            dprob = matmul_last(v_ref[keys, :], g_rows)
            dscore = prob * (dprob - delta).astype(BF16)
            dv_acc[keys, :] += matmul(prob, g_rows)
            dk_acc[keys, :] += matmul(dscore, q_rows)
            out_turned += matmul_first(v_ref[keys, :], prob)
            dq_turned += matmul_first(k_ref[keys, :], dscore)
        out_ref[:, rows] = out_turned.astype(BF16)
        dq_ref[:, rows] = dq_turned.astype(BF16)

    dkv_ref[0] = (dk_acc[...] * scale).astype(BF16)
    dkv_ref[1] = dv_acc[...].astype(BF16)


def holders(tile_of_ref, holder):
    n_ctx = tile_of_ref.shape[0]
    for ctx in range(n_ctx):
        holder[tile_of_ref[ctx]] = ctx


def route_kernel(window, place_ref, tile_of_ref, held_ref, out_ref, holder):
    group, n_head = out_ref.shape[:2]
    holders(tile_of_ref, holder)
    first = lax.div(place_ref[0], group) * group

    def one(member, carry):
        for slot in range(window):
            tile = tile_of_ref[first + member] - (window - slot)
            source = holder[jnp.maximum(tile, 0)]
            rows = held_ref[source]
            for head in range(n_head):
                out_ref[member, head, slot] = rows
        return carry

    lax.fori_loop(0, group, one, 0)


def sum_kernel(window, group, place_ref, tile_of_ref, terms_ref, order_ref, out_ref, holder):
    n_ctx, n_head = out_ref.shape[:2]
    holders(tile_of_ref, holder)
    first = lax.div(place_ref[0], group) * group

    def one(ctx, carry):
        total = jnp.zeros(out_ref.shape[2:], F32)
        for slot in range(window):
            tile = tile_of_ref[ctx] + (window - slot)
            source = holder[jnp.minimum(tile, n_ctx - 1)] - first
            here = (tile < n_ctx) & (source >= 0) & (source < group)
            source = jnp.where(here, source, 0)
            part = terms_ref[source, 0, slot].astype(F32)
            for head in range(1, n_head):
                part = part + terms_ref[source, head, slot].astype(F32)
            total = total + jnp.where(here, part, 0.0)
        for head in range(n_head):
            out_ref[ctx, head] = total.astype(BF16)
        return carry

    lax.fori_loop(0, n_ctx, one, 0)


def shape_of(shape, dtype):
    return jax.ShapeDtypeStruct(shape, dtype)


def call(body, name, scalars, arrays, out_shape, scratch, flops, space=VMEM):
    return pl.pallas_call(
        body,
        in_specs=[SMEM] * scalars + [space] * arrays,
        out_specs=(space,) * len(out_shape),
        out_shape=out_shape,
        scratch_shapes=scratch,
        compiler_params=pltpu.CompilerParams(vmem_limit_bytes=VMEM_LIMIT),
        cost_estimate=pl.CostEstimate(
            flops=flops, bytes_accessed=1 << 22, transcendentals=0
        ),
        name=name,
    )


def past_call(window, heads, pieces_shape, row_total, work):
    n_owners, _, _, piece, width = pieces_shape
    past_rows = window * n_owners * piece
    chunks = row_total // ROW_BLOCK
    rows = pltpu.VMEM((row_total, width), BF16)
    stats = pltpu.VMEM((8, row_total), F32)
    win = pltpu.VMEM((2, window, n_owners, piece, width), BF16)
    acc = pltpu.VMEM((past_rows, width), F32)
    dma = pltpu.SemaphoreType.DMA
    return call(
        functools.partial(past_kernel, window, heads),
        "past",
        3,
        4,
        (shape_of((8, row_total), F32), shape_of(pieces_shape, BF16)),
        [
            rows,
            rows,
            stats,
            stats,
            win,
            win,
            acc,
            acc,
            dma((chunks, 2)),
            dma((2, window)),
            dma((2,)),
            dma((2, window)),
        ],
        4 * window * work,
        HBM,
    )


def late_call(window, heads, pieces_shape, row_total, work):
    n_owners, _, _, piece, width = pieces_shape
    chunks = row_total // ROW_BLOCK
    rows = pltpu.VMEM((row_total, width), BF16)
    columns = pltpu.VMEM((width, row_total), BF16)
    dma = pltpu.SemaphoreType.DMA
    return call(
        functools.partial(late_kernel, window, heads),
        "late",
        3,
        7,
        (shape_of((row_total, width), BF16), shape_of((row_total, width), BF16)),
        [
            rows,
            rows,
            pltpu.VMEM((8, row_total), F32),
            pltpu.VMEM((2, window, n_owners, piece, width), BF16),
            columns,
            columns,
            rows,
            rows,
            dma((chunks, 4)),
            dma((2, window)),
            dma((1,)),
            dma((chunks, 2)),
        ],
        4 * window * work,
        HBM,
    )


def own_forward_call(heads, tile_rows, width, row_total, work):
    chunk_pos = ROW_BLOCK // heads
    ends = range(chunk_pos, tile_rows + 1, chunk_pos)
    return call(
        functools.partial(own_forward_kernel, heads),
        "own_forward",
        3,
        4,
        (shape_of((8, row_total), F32),) + tuple(shape_of((end, ROW_BLOCK), BF16) for end in ends),
        [],
        2 * work,
    )


def own_grads_call(heads, tile_rows, width, row_total, work):
    return call(
        functools.partial(own_grads_kernel, heads),
        "own_grads",
        0,
        5 + row_total // ROW_BLOCK,
        (
            shape_of((width, row_total), BF16),
            shape_of((width, row_total), BF16),
            shape_of((2, tile_rows, width), BF16),
        ),
        [pltpu.VMEM((tile_rows, width), F32), pltpu.VMEM((tile_rows, width), F32)],
        4 * work,
    )


def small_call(body, name, out_shape, n_ctx, ordered=0):
    return pl.pallas_call(
        body,
        in_specs=[SMEM, SMEM, VMEM] + [HBM] * ordered,
        out_specs=VMEM,
        out_shape=out_shape,
        scratch_shapes=[pltpu.SMEM((n_ctx,), jnp.int32)],
        compiler_params=pltpu.CompilerParams(vmem_limit_bytes=SMALL_LIMIT),
        name=name,
    )


def on_device(queries, keys, values, grad_out, lengths, tile_of):
    tile_rows, heads, width = queries.shape
    n_ctx = lax.axis_size("ctx")
    n_head = lax.axis_size("head")
    group = n_ctx // 2
    n_owners = group * n_head
    piece = tile_rows // n_owners
    both = ("ctx", "head")
    halves = [list(range(n_owners)), list(range(n_owners, 2 * n_owners))]
    most_doc = n_ctx * tile_rows // 8
    window = -(-(most_doc - 1) // tile_rows)
    row_total = tile_rows * heads
    place = lax.axis_index("ctx").astype(jnp.int32).reshape(1)
    y = lax.axis_index("head")
    scalars = (place, lengths, tile_of)
    q_rows = queries.reshape(row_total, width)
    g_rows = grad_out.reshape(row_total, width)
    work = 2 * row_total * tile_rows * width
    fine = piece % 16 == 0

    pieces = jnp.stack(
        [tile.reshape(group, n_head, piece, width) for tile in (keys, values)], axis=2
    )
    mine = lax.dynamic_index_in_dim(pieces, y, 1, keepdims=False)
    held = lax.all_to_all(jnp.concatenate([mine, mine]), "ctx", 0, 0, tiled=True)
    packed = small_call(
        functools.partial(route_kernel, window),
        "route",
        shape_of((group, n_head, window, 2, piece, width), BF16),
        n_ctx,
    )(place, tile_of, held)
    past = lax.all_to_all(
        packed.reshape(n_owners, window, 2, piece, width),
        both,
        0,
        0,
        tiled=True,
        axis_index_groups=halves,
    )
    pieces_shape = (n_owners, window, 2, piece, width)
    if not fine:
        pieces_shape = (1, window, 2, tile_rows, width)
        past = past.transpose(1, 2, 0, 3, 4).reshape(pieces_shape)

    own_stats, *own_weights = own_forward_call(heads, tile_rows, width, row_total, work)(
        *scalars, q_rows, g_rows, keys, values
    )
    stats, terms = past_call(window, heads, pieces_shape, row_total, work)(
        *scalars, q_rows, g_rows, own_stats, past
    )
    own_out, own_dq, own_grads = own_grads_call(heads, tile_rows, width, row_total, work)(
        q_rows, g_rows, stats, keys, values, *own_weights
    )

    if not fine:
        terms = terms.reshape(window, 2, n_owners, piece, width).transpose(2, 0, 1, 3, 4)
    terms = lax.all_to_all(terms, both, 0, 0, tiled=True, axis_index_groups=halves)
    summed = small_call(
        functools.partial(sum_kernel, window, group),
        "sum_terms",
        shape_of((n_ctx, n_head, 2, piece, width), BF16),
        n_ctx,
        1,
    )(place, tile_of, terms.reshape(group, n_head, window, 2, piece, width), own_grads)
    summed = summed.reshape(n_ctx * n_head, 2, piece, width)
    far = lax.all_to_all(summed, both, 0, 0, tiled=True)
    attended, query_grad = late_call(window, heads, pieces_shape, row_total, work)(
        *scalars, q_rows, g_rows, stats, past, own_out, own_dq, summed
    )

    if n_head == 2:
        peer = lax.ppermute(own_grads, "head", [(0, 1), (1, 0)])
        peer, far, attended = lax.optimization_barrier((peer, far, attended))
        near = own_grads.astype(F32) + peer.astype(F32)
    else:
        near = lax.psum(own_grads.astype(F32), "head")
    far = far.reshape(2, n_owners, 2, piece, width).astype(F32)
    far = far[0] + far[1]
    far_keys, far_values = (far[:, part].reshape(tile_rows, width) for part in range(2))
    return (
        attended.reshape(tile_rows, heads, width),
        query_grad.reshape(tile_rows, heads, width),
        near[0] + far_keys,
        near[1] + far_values,
    )


def solution(mesh):
    return jax.shard_map(
        on_device,
        mesh=mesh,
        in_specs=(
            P("ctx", "head", None),
            P("ctx", None),
            P("ctx", None),
            P("ctx", "head", None),
            P(),
            P(),
        ),
        out_specs=(P("ctx", "head", None), P("ctx", "head", None), P("ctx", None), P("ctx", None)),
        check_vma=False,
    )
```

profile of v0, /device:TPU:0, one launch (start us, length us, event | category | flops | bytes accessed | tf_op | source)
XLA Modules:
  0.0 83.6 jit_solution(5470778795475444884)
XLA Ops:
  0.6 0.9 %copy_bitcast_fusion = bf16[8,2,32,128]{3,2,1,0:T(8,128)(2,1)S(1)} fusion(s32[]{:T(128)S(6)} %select_n.4, bf16[8,2,1,32,128]{4,3,1,0,2:T(8,128)(2,1)} %bitcast.25, bf16[8,2,1,32,128]{4,3,1,0,2:T(8,128)(2,1)} %bitcast.26), kind=kLoop, calls=%fused_computation.10 | loop fusion | flops 65536 | bytes 393220 | tf_op jit(solution)/shard_map/jit(dynamic_index_in_dim)/squeeze | solution.py:632
  1.5 0.7 pad_maximum_fusion
  2.2 7.4 %all-to-all-start = ((bf16[16,2,32,128]{3,2,1,0:T(8,128)(2,1)}), bf16[16,2,32,128]{3,2,1,0:T(8,128)(2,1)S(1)}, u32[]{:S(2)}, u32[]{:S(2)}) async-start(bf16[16,2,32,128]{3,2,1,0:T(8,128)(2,1)} %pad_maximum_fusion), calls=%async_computation | async-start | bytes 524288 | tf_op jit(solution)/shard_map/all_to_all | solution.py:633
  9.6 0.0 copy-start.2
  9.6 10.0 %all-to-all-done.held_ref = bf16[16,2,32,128]{3,2,1,0:T(8,128)(2,1)S(1)} async-done(((bf16[16,2,32,128]{3,2,1,0:T(8,128)(2,1)}), bf16[16,2,32,128]{3,2,1,0:T(8,128)(2,1)S(1)}, u32[]{:S(2)}, u32[]{:S(2)}) %all-to-all-start) | async-done | bytes 262176 | tf_op jit(solution)/shard_map/all_to_all | solution.py:633
  19.7 0.0 copy-done.2
  19.7 1.5 %route.1 = bf16[8,2,2,2,32,128]{5,4,3,2,1,0:T(8,128)(2,1)} custom-call(s32[1]{0:T(128)} %bitcast.2.place_ref, s32[16]{0:T(128)S(1)} %copy-done.2, bf16[16,2,32,128]{3,2,1,0:T(8,128)(2,1)S(1)} %all-to-all-done.held_ref), custom_call_target="tpu_custom_call" | custom-call | tf_op jit(solution)/shard_map/route/pallas_call | solution.py:634
  21.2 3.6 %all-to-all-start.1 = ((bf16[16,2,2,32,128]{4,3,2,1,0:T(8,128)(2,1)}), bf16[16,2,2,32,128]{4,3,2,1,0:T(8,128)(2,1)S(1)}, u32[]{:S(2)}, u32[]{:S(2)}) async-start(bf16[16,2,2,32,128]{4,3,2,1,0:T(8,128)(2,1)} %bitcast.6), calls=%async_computation.1 | async-start | bytes 1048576 | tf_op jit(solution)/shard_map/all_to_all | solution.py:640
  24.8 5.4 %own_forward.1 = (f32[8,4096]{1,0:T(8,128)}, bf16[128,1024]{1,0:T(8,128)(2,1)}, bf16[256,1024]{1,0:T(8,128)(2,1)}, bf16[384,1024]{1,0:T(8,128)(2,1)}, bf16[512,1024]{1,0:T(8,128)(2,1)}) custom-call(s32[1]{0:T(128)} %bitcast.2.place_ref, s32[16]{0:T(128)} %lengths_ref.5, s32[16]{0:T(128)} %tile_of_ref.9, bf16[4096,128]{1,0:T(8,128)(2,1)} %bitcast.27, ...), custom_call_target="tpu_custom_call" | custom-call | flops 1073741824 | bytes 4194304 | tf_op jit(solution)/shard_map/own_forward/pallas_call | solution.py:653
  30.2 4.1 %all-to-all-done.1.past_hbm = bf16[16,2,2,32,128]{4,3,2,1,0:T(8,128)(2,1)S(1)} async-done(((bf16[16,2,2,32,128]{4,3,2,1,0:T(8,128)(2,1)}), bf16[16,2,2,32,128]{4,3,2,1,0:T(8,128)(2,1)S(1)}, u32[]{:S(2)}, u32[]{:S(2)}) %all-to-all-start.1) | async-done | bytes 524320 | tf_op jit(solution)/shard_map/all_to_all | solution.py:640
  34.3 0.0 copy-start.4
  34.3 0.8 copy-done.4
  35.1 6.3 %past.1 = (f32[8,4096]{1,0:T(8,128)}, bf16[16,2,2,32,128]{4,3,2,1,0:T(8,128)(2,1)}) custom-call(s32[1]{0:T(128)} %bitcast.2.place_ref, s32[16]{0:T(128)} %lengths_ref.5, s32[16]{0:T(128)} %tile_of_ref.9, bf16[4096,128]{1,0:T(8,128)(2,1)} %bitcast.28, bf16[4096,128]{1,0:T(8,128)(2,1)} %bitcast.32, f32[8,4096]{1,0:T(8,128)} %get-tuple-element.19.own_stats_hbm, ...), custom_call_target="tpu_custom_call" | custom-call | flops 4294967296 | bytes 4194304 | tf_op jit(solution)/shard_map/past/pallas_call | solution.py:656
  41.4 7.7 %all-to-all-start.2 = ((bf16[16,2,2,32,128]{4,3,2,1,0:T(8,128)(2,1)}), bf16[16,2,2,32,128]{4,3,2,1,0:T(8,128)(2,1)S(1)}, u32[]{:S(2)}, u32[]{:S(2)}) async-start(bf16[16,2,2,32,128]{4,3,2,1,0:T(8,128)(2,1)} %get-tuple-element.26), calls=%async_computation.2 | async-start | bytes 1048576 | tf_op jit(solution)/shard_map/all_to_all | solution.py:665
  49.1 6.8 %own_grads.1 = (bf16[128,4096]{1,0:T(8,128)(2,1)}, bf16[128,4096]{1,0:T(8,128)(2,1)}, bf16[2,512,128]{2,1,0:T(8,128)(2,1)}) custom-call(bf16[4096,128]{1,0:T(8,128)(2,1)} %bitcast.29, bf16[4096,128]{1,0:T(8,128)(2,1)} %bitcast.33, f32[8,4096]{1,0:T(8,128)} %get-tuple-element.20.stats_ref.stats_hbm, bf16[512,128]{1,0:T(8,128)(2,1)} %k_ref.3, ...), custom_call_target="tpu_custom_call" | custom-call | flops 2147483648 | bytes 4194304 | tf_op jit(solution)/shard_map/own_grads/pallas_call | solution.py:659
  55.9 3.2 %all-to-all-done.2 = bf16[16,2,2,32,128]{4,3,2,1,0:T(8,128)(2,1)S(1)} async-done(((bf16[16,2,2,32,128]{4,3,2,1,0:T(8,128)(2,1)}), bf16[16,2,2,32,128]{4,3,2,1,0:T(8,128)(2,1)S(1)}, u32[]{:S(2)}, u32[]{:S(2)}) %all-to-all-start.2) | async-done | bytes 524320 | tf_op jit(solution)/shard_map/all_to_all | solution.py:665
  59.1 0.0 copy-start.3
  59.1 0.7 copy-done.3
  59.8 0.0 copy-start
  59.8 0.9 %copy-done = bf16[2,512,128]{2,1,0:T(8,128)(2,1)S(1)} copy-done((bf16[2,512,128]{2,1,0:T(8,128)(2,1)S(1)}, bf16[2,512,128]{2,1,0:T(8,128)(2,1)}, u32[]{:S(2)}) %copy-start) | copy-done | bytes 262168
  60.7 1.8 %sum_terms.1 = bf16[16,2,2,32,128]{4,3,2,1,0:T(8,128)(2,1)} custom-call(s32[1]{0:T(128)} %bitcast.2.place_ref, s32[16]{0:T(128)S(1)} %copy-done.3, bf16[8,2,2,2,32,128]{5,4,3,2,1,0:T(8,128)(2,1)S(1)} %bitcast.24, bf16[2,512,128]{2,1,0:T(8,128)(2,1)S(1)} %copy-done), custom_call_target="tpu_custom_call" | custom-call | tf_op jit(solution)/shard_map/sum_terms/pallas_call | solution.py:666
  62.5 0.0 copy-start.1
  62.5 4.9 %all-to-all-start.3 = ((bf16[32,2,32,128]{3,2,1,0:T(8,128)(2,1)}), bf16[32,2,32,128]{3,2,1,0:T(8,128)(2,1)S(1)}, u32[]{:S(2)}, u32[]{:S(2)}) async-start(bf16[32,2,32,128]{3,2,1,0:T(8,128)(2,1)} %bitcast.8.summed_hbm), calls=%async_computation.3 | async-start | bytes 1048576 | tf_op jit(solution)/shard_map/all_to_all | solution.py:674
  67.4 0.0 copy-done.1
  67.4 1.8 %collective-permute-start = (bf16[2,512,128]{2,1,0:T(8,128)(2,1)S(1)}, bf16[2,512,128]{2,1,0:T(8,128)(2,1)S(1)}, u32[]{:S(2)}, u32[]{:S(2)}) collective-permute-start(bf16[2,512,128]{2,1,0:T(8,128)(2,1)S(1)} %copy-done.1), channel_id=1, source_target_pairs={{0,1},{1,0},{2,3},{3,2},{4,5},{5,4},{6,7},{7,6},{8,9},{9,8},{10,11... | collective-permute-start | bytes 786440 | tf_op jit(solution)/shard_map/ppermute | solution.py:680
  69.3 7.1 %late.1 = (bf16[4096,128]{1,0:T(8,128)(2,1)}, bf16[4096,128]{1,0:T(8,128)(2,1)}) custom-call(s32[1]{0:T(128)} %bitcast.2.place_ref, s32[16]{0:T(128)} %lengths_ref.5, s32[16]{0:T(128)} %tile_of_ref.9, bf16[4096,128]{1,0:T(8,128)(2,1)} %bitcast.30, bf16[4096,128]{1,0:T(8,128)(2,1)} %bitcast.34, f32[8,4096]{1,0:T(8,128)} %get-tuple-element.20.stats_ref.stats_hbm, ...), custom_call_target="tpu_custom_call" | custom-call | flops 4294967296 | bytes 4194304 | tf_op jit(solution)/shard_map/late/pallas_call | solution.py:675
  76.4 4.2 %collective-permute-done = bf16[2,512,128]{2,1,0:T(8,128)(2,1)S(1)} collective-permute-done((bf16[2,512,128]{2,1,0:T(8,128)(2,1)S(1)}, bf16[2,512,128]{2,1,0:T(8,128)(2,1)S(1)}, u32[]{:S(2)}, u32[]{:S(2)}) %collective-permute-start) | collective-permute-done | bytes 262176 | tf_op jit(solution)/shard_map/ppermute | solution.py:680
  80.6 1.8 %all-to-all-done.3 = bf16[32,2,32,128]{3,2,1,0:T(8,128)(2,1)S(1)} async-done(((bf16[32,2,32,128]{3,2,1,0:T(8,128)(2,1)}), bf16[32,2,32,128]{3,2,1,0:T(8,128)(2,1)S(1)}, u32[]{:S(2)}, u32[]{:S(2)}) %all-to-all-start.3) | async-done | bytes 524320 | tf_op jit(solution)/shard_map/all_to_all | solution.py:674
  82.4 0.1 convert_add_fusion
  82.5 0.1 convert_element_type.12
  82.6 0.1 slice_add_fusion
  82.7 0.8 %fusion = (f32[512,128]{1,0:T(8,128)}, f32[512,128]{1,0:T(8,128)}) fusion(f32[2,512,128]{2,1,0:T(8,128)S(1)} %convert_add_fusion, f32[16,1,32,128]{3,2,1,0:T(8,128)S(1)} %get-tuple-element.36, f32[16,1,32,128]{3,2,1,0:T(8,128)S(1)} %get-tuple-element.37), kind=kLoop, calls=%fused_computation.3 | loop fusion | flops 131072 | bytes 1572864 | tf_op jit(solution)/shard_map/add | solution.py:692
  (1 shorter events, 0.0 us)
Async XLA Ops:
  2.2 17.4 %all-to-all-start = ((bf16[16,2,32,128]{3,2,1,0:T(8,128)(2,1)}), bf16[16,2,32,128]{3,2,1,0:T(8,128)(2,1)S(1)}, u32[]{:S(2)}, u32[]{:S(2)}) async-start(bf16[16,2,32,128]{3,2,1,0:T(8,128)(2,1)} %pad_maximum_fusion), calls=%async_computation | async-start | bytes 524288 | tf_op jit(solution)/shard_map/all_to_all | solution.py:633
  9.6 10.0 %copy-start.2 = (s32[16]{0:T(128)S(1)}, s32[16]{0:T(128)}, u32[]{:S(2)}) copy-start(s32[16]{0:T(128)} %tile_of_ref.9) | copy-start | bytes 196
  21.2 13.1 %all-to-all-start.1 = ((bf16[16,2,2,32,128]{4,3,2,1,0:T(8,128)(2,1)}), bf16[16,2,2,32,128]{4,3,2,1,0:T(8,128)(2,1)S(1)}, u32[]{:S(2)}, u32[]{:S(2)}) async-start(bf16[16,2,2,32,128]{4,3,2,1,0:T(8,128)(2,1)} %bitcast.6), calls=%async_computation.1 | async-start | bytes 1048576 | tf_op jit(solution)/shard_map/all_to_all | solution.py:640
  34.3 0.8 copy-start.4
  41.4 17.7 %all-to-all-start.2 = ((bf16[16,2,2,32,128]{4,3,2,1,0:T(8,128)(2,1)}), bf16[16,2,2,32,128]{4,3,2,1,0:T(8,128)(2,1)S(1)}, u32[]{:S(2)}, u32[]{:S(2)}) async-start(bf16[16,2,2,32,128]{4,3,2,1,0:T(8,128)(2,1)} %get-tuple-element.26), calls=%async_computation.2 | async-start | bytes 1048576 | tf_op jit(solution)/shard_map/all_to_all | solution.py:665
  59.1 0.7 copy-start.3
  59.8 0.9 %copy-start = (bf16[2,512,128]{2,1,0:T(8,128)(2,1)S(1)}, bf16[2,512,128]{2,1,0:T(8,128)(2,1)}, u32[]{:S(2)}) copy-start(bf16[2,512,128]{2,1,0:T(8,128)(2,1)} %get-tuple-element.25.order_ref) | copy-start | bytes 786436
  62.5 4.9 %copy-start.1 = (bf16[2,512,128]{2,1,0:T(8,128)(2,1)S(1)}, bf16[2,512,128]{2,1,0:T(8,128)(2,1)}, u32[]{:S(2)}) copy-start(bf16[2,512,128]{2,1,0:T(8,128)(2,1)} %get-tuple-element.25.order_ref) | copy-start | bytes 786436
  62.5 19.9 %all-to-all-start.3 = ((bf16[32,2,32,128]{3,2,1,0:T(8,128)(2,1)}), bf16[32,2,32,128]{3,2,1,0:T(8,128)(2,1)S(1)}, u32[]{:S(2)}, u32[]{:S(2)}) async-start(bf16[32,2,32,128]{3,2,1,0:T(8,128)(2,1)} %bitcast.8.summed_hbm), calls=%async_computation.3 | async-start | bytes 1048576 | tf_op jit(solution)/shard_map/all_to_all | solution.py:674
  67.4 13.2 %collective-permute-start = (bf16[2,512,128]{2,1,0:T(8,128)(2,1)S(1)}, bf16[2,512,128]{2,1,0:T(8,128)(2,1)S(1)}, u32[]{:S(2)}, u32[]{:S(2)}) collective-permute-start(bf16[2,512,128]{2,1,0:T(8,128)(2,1)S(1)} %copy-done.1), channel_id=1, source_target_pairs={{0,1},{1,0},{2,3},{3,2},{4,5},{5,4},{6,7},{7,6},{8,9},{9,8},{10,11... | collective-permute-start | bytes 786440 | tf_op jit(solution)/shard_map/ppermute | solution.py:680
where the time goes:
time: 83.9 us; the launch traced here: 83.6 us
  Pallas kernels  29 us (35%)
  starting transfers between devices  25.3 us (30%)
  waiting for transfers between devices  23.4 us (28%)
  other arithmetic  2.72 us (3%)
  local copies, waits for them, and re-layouts  2.45 us (3%)
    all_to_all x1, waiting for transfers between devices, on_device(): lax.all_to_all(jnp.concatenate([mine, mine]), 'ctx', 0, 0, tiled=True)  10 us
    all_to_all x1, starting transfers between devices, on_device(): lax.all_to_all(terms, both, 0, 0, tiled=True, axis_index_groups=halves)  7.67 us
    all_to_all x1, starting transfers between devices, on_device(): lax.all_to_all(jnp.concatenate([mine, mine]), 'ctx', 0, 0, tiled=True)  7.36 us
    pallas_call x1, Pallas kernels, on_device(): late_call(window, heads, pieces_shape, row_total, work)  7.15 us
    pallas_call x1, Pallas kernels, on_device(): own_grads_call(heads, tile_rows, width, row_total, work)  6.76 us
    pallas_call x1, Pallas kernels, on_device(): past_call(window, heads, pieces_shape, row_total, work)  6.3 us
    pallas_call x1, Pallas kernels, on_device(): own_forward_call(heads, tile_rows, width, row_total, work)  5.44 us
    all_to_all x1, starting transfers between devices, on_device(): far = lax.all_to_all(summed, both, 0, 0, tiled=True)  4.88 us
  transfers between devices with their start and end apart: 5, of which 5 were waited for; matrix products, arithmetic and copies ran while one was open for 0% of the time, Pallas kernels for 23%

commit v1 on v0

--- a/solution.py
+++ b/solution.py
@@ -13,9 +13,12 @@
 ROW_BLOCK = 1024
 VMEM_LIMIT = 60 * 1024 * 1024
 SMALL_LIMIT = 16 * 1024 * 1024
+PAST_LIMIT = 52 * 1024 * 1024
+STATS_SIZE = 1 << 22
 SMEM = pl.BlockSpec(memory_space=pltpu.SMEM)
 VMEM = pl.BlockSpec(memory_space=pltpu.VMEM)
-HBM = pl.BlockSpec(memory_space=pl.ANY)
+ANY = pl.BlockSpec(memory_space=pl.ANY)
+HBM = pl.BlockSpec(memory_space=pltpu.HBM)
 F32 = jnp.float32
 BF16 = jnp.bfloat16
 
@@ -83,8 +86,9 @@
 
 
 def own_forward_kernel(
-    heads, place_ref, lengths_ref, tile_of_ref, q_ref, g_ref, k_ref, v_ref, stats_ref, *weight_refs
+    heads, place_ref, lengths_ref, tile_of_ref, q_ref, g_ref, k_ref, v_ref, stats_hbm, *refs
 ):
+    *weight_refs, stats_ref, stats_sem = refs
     tile_rows, width = k_ref.shape
     exponent_scale = float(width) ** (-0.5) * LOG2E
     chunk_pos = ROW_BLOCK // heads
@@ -118,10 +122,26 @@
         stats_ref[1:2, rows] = jnp.sum(sums, axis=0, keepdims=True)
         stats_ref[2:3, rows] = jnp.sum(products, axis=0, keepdims=True)
 
+    first_start, first_end = crossing(ends, tile_begin)
+    for row, value in ((3, tile_begin), (4, first_start), (5, first_end)):
+        stats_ref[row : row + 1, :] = jnp.full((1, stats_ref.shape[1]), value, jnp.int32).astype(F32)
+    stats_out = pltpu.make_async_copy(stats_ref, stats_hbm.at[0:8], stats_sem.at[0])
+    stats_out.start()
+    stats_out.wait()
+
+
+def crossing(ends, tile_begin):
+    first_start, first_end = jnp.int32(0), jnp.int32(0)
+    for end in ends:
+        crosses = (first_end <= tile_begin) & (end > tile_begin)
+        first_start = jnp.where(end <= tile_begin, end, first_start)
+        first_end = jnp.where(crosses, end, first_end)
+    return first_start, first_end
+
 
 class Past:
-    def __init__(self, window, heads, place_ref, lengths_ref, tile_of_ref, past_hbm, win_ref):
-        n_owners, _, _, self.piece, self.width = past_hbm.shape
+    def __init__(self, window, heads, past_hbm, win_ref):
+        _, _, n_owners, self.piece, self.width = win_ref.shape
         self.n_owners = n_owners
         self.tile_rows = n_owners * self.piece
         self.past_rows = window * self.tile_rows
@@ -130,15 +150,13 @@
         self.window = window
         self.past_hbm = past_hbm
         self.win_ref = win_ref
-        self.tile_begin = tile_of_ref[place_ref[0]] * self.tile_rows
-        first_start, self.first_end = jnp.int32(0), jnp.int32(0)
-        for end in document_ends(lengths_ref):
-            crosses = (self.first_end <= self.tile_begin) & (end > self.tile_begin)
-            first_start = jnp.where(end <= self.tile_begin, end, first_start)
-            self.first_end = jnp.where(crosses, end, self.first_end)
-        self.first_key = jnp.maximum(self.past_rows - (self.tile_begin - first_start), 0)
         self.unit = window * KEY_BLOCK // 4
         self.branches = self.past_rows // self.unit
+
+    def plan(self, stats_ref):
+        plan = [jnp.max(stats_ref[row : row + 1, 0:128]).astype(jnp.int32) for row in (3, 4, 5)]
+        self.tile_begin, first_start, self.first_end = plan
+        self.first_key = jnp.maximum(self.past_rows - (self.tile_begin - first_start), 0)
         self.all_units = self.branches - lax.div(self.first_key, self.unit)
 
     def copies(self, part, sem):
@@ -213,15 +231,14 @@
 def past_kernel(
     window,
     heads,
-    place_ref,
-    lengths_ref,
-    tile_of_ref,
     q_hbm,
     g_hbm,
     own_stats_hbm,
     past_hbm,
+    kept_in_hbm,
     stats_hbm,
     terms_hbm,
+    kept_hbm,
     q_ref,
     g_ref,
     own_stats_ref,
@@ -234,15 +251,16 @@
     past_sem,
     stats_sem,
     terms_sem,
+    kept_sem,
 ):
-    past = Past(window, heads, place_ref, lengths_ref, tile_of_ref, past_hbm, win_ref)
+    past = Past(window, heads, past_hbm, win_ref)
     past_rows, width = dk_acc.shape
     scale = float(width) ** (-0.5)
     exponent_scale = scale * LOG2E
     chunks = q_ref.shape[0] // ROW_BLOCK
     pairs = ((q_hbm, q_ref, 0), (g_hbm, g_ref, 0))
-    stats_in = pltpu.make_async_copy(own_stats_hbm, own_stats_ref, stats_sem.at[0])
-    stats_out = pltpu.make_async_copy(stats_ref, stats_hbm, stats_sem.at[1])
+    stats_in = pltpu.make_async_copy(own_stats_hbm.at[0:8], own_stats_ref, stats_sem.at[0])
+    stats_out = pltpu.make_async_copy(stats_ref, stats_hbm.at[0:8], stats_sem.at[1])
 
     start_all(past.copies(0, past_sem))
     start_all(chunk_copies(pairs, in_sem, 0))
@@ -253,6 +271,16 @@
     dk_acc[...] = jnp.zeros_like(dk_acc)
     dv_acc[...] = jnp.zeros_like(dv_acc)
     wait_all(past.copies(0, past_sem) + past.copies(1, past_sem) + [stats_in])
+    past.plan(own_stats_ref)
+    stats_ref[3:6, :] = own_stats_ref[3:6, :]
+    keep = [
+        pltpu.make_async_copy(
+            win_ref.at[part, slot], kept_hbm.at[:, slot, part], kept_sem.at[part, slot]
+        )
+        for part in range(2)
+        for slot in range(window)
+    ]
+    start_all(keep)
 
     def chunk_step(chunk, carry):
         rows = chunk_rows(chunk)
@@ -305,7 +333,7 @@
 
     lax.fori_loop(0, chunks, chunk_step, 0)
     stats_out.start()
-    copies = [stats_out]
+    copies = [stats_out] + keep
     for slot in range(window):
         rows = slice(slot * past.tile_rows, (slot + 1) * past.tile_rows)
         shape = (past.n_owners, past.piece, width)
@@ -323,9 +351,6 @@
 def late_kernel(
     window,
     heads,
-    place_ref,
-    lengths_ref,
-    tile_of_ref,
     q_hbm,
     g_hbm,
     stats_hbm,
@@ -348,7 +373,7 @@
     stats_sem,
     out_sem,
 ):
-    past = Past(window, heads, place_ref, lengths_ref, tile_of_ref, past_hbm, win_ref)
+    past = Past(window, heads, past_hbm, win_ref)
     width = past.width
     scale = float(width) ** (-0.5)
     exponent_scale = scale * LOG2E
@@ -360,11 +385,13 @@
         (own_dq_hbm, own_dq_ref, 1),
     )
     out_pairs = ((att_ref, att_hbm, 0), (dq_ref, dq_hbm, 0))
-    stats_in = pltpu.make_async_copy(stats_hbm, stats_ref, stats_sem.at[0])
-    start_all(past.copies(0, past_sem) + past.copies(1, past_sem) + [stats_in])
+    stats_in = pltpu.make_async_copy(stats_hbm.at[0:8], stats_ref, stats_sem.at[0])
+    window_in = past.copies(0, past_sem) + past.copies(1, past_sem) + [stats_in]
+    start_all(window_in)
     for chunk in range(chunks):
         start_all(chunk_copies(pairs, in_sem, chunk))
-    wait_all(past.copies(0, past_sem) + past.copies(1, past_sem) + [stats_in])
+    wait_all(window_in)
+    past.plan(stats_ref)
 
     def chunk_step(chunk, carry):
         rows = chunk_rows(chunk)
@@ -401,16 +428,19 @@
 
 
 def own_grads_kernel(
-    heads, q_ref, g_ref, stats_ref, k_ref, v_ref, *refs
+    heads, q_ref, g_ref, stats_hbm, k_ref, v_ref, *refs
 ):
     tile_rows, width = k_ref.shape
     chunk_pos = ROW_BLOCK // heads
     chunks = q_ref.shape[0] // ROW_BLOCK
     weight_refs = refs[:chunks]
-    out_ref, dq_ref, dkv_ref, dk_acc, dv_acc = refs[chunks:]
+    out_ref, dq_ref, dkv_ref, stats_ref, stats_sem, dk_acc, dv_acc = refs[chunks:]
     scale = float(width) ** (-0.5)
+    stats_in = pltpu.make_async_copy(stats_hbm.at[0:8], stats_ref, stats_sem.at[0])
+    stats_in.start()
     dk_acc[...] = jnp.zeros_like(dk_acc)
     dv_acc[...] = jnp.zeros_like(dv_acc)
+    stats_in.wait()
 
     for chunk, rows in enumerate(row_blocks(q_ref.shape[0])):
         rescale = stats_ref[0:1, rows]
@@ -440,30 +470,30 @@
         holder[tile_of_ref[ctx]] = ctx
 
 
-def route_kernel(window, place_ref, tile_of_ref, held_ref, out_ref, holder):
-    group, n_head = out_ref.shape[:2]
+def route_kernel(window, place_ref, tile_of_ref, held_hbm, out_hbm, holder, sem):
+    group, n_head = out_hbm.shape[:2]
     holders(tile_of_ref, holder)
     first = lax.div(place_ref[0], group) * group
-
-    def one(member, carry):
+    for member in range(group):
         for slot in range(window):
             tile = tile_of_ref[first + member] - (window - slot)
             source = holder[jnp.maximum(tile, 0)]
-            rows = held_ref[source]
             for head in range(n_head):
-                out_ref[member, head, slot] = rows
-        return carry
-
-    lax.fori_loop(0, group, one, 0)
-
-
-def sum_kernel(window, group, place_ref, tile_of_ref, terms_ref, order_ref, out_ref, holder):
-    n_ctx, n_head = out_ref.shape[:2]
+                pltpu.make_async_copy(
+                    held_hbm.at[source], out_hbm.at[member, head, slot], sem.at[member]
+                ).start()
+    for member in range(group):
+        whole = out_hbm.at[member]
+        pltpu.make_async_copy(whole, whole, sem.at[member]).wait()
+
+
+def sum_kernel(window, group, place_ref, tile_of_ref, terms_ref, out_hbm, holder, summed, sem):
+    n_ctx, n_head = out_hbm.shape[:2]
     holders(tile_of_ref, holder)
     first = lax.div(place_ref[0], group) * group
 
     def one(ctx, carry):
-        total = jnp.zeros(out_ref.shape[2:], F32)
+        total = jnp.zeros(summed.shape[1:], F32)
         for slot in range(window):
             tile = tile_of_ref[ctx] + (window - slot)
             source = holder[jnp.minimum(tile, n_ctx - 1)] - first
@@ -473,30 +503,38 @@
             for head in range(1, n_head):
                 part = part + terms_ref[source, head, slot].astype(F32)
             total = total + jnp.where(here, part, 0.0)
+        summed[ctx] = total.astype(BF16)
         for head in range(n_head):
-            out_ref[ctx, head] = total.astype(BF16)
+            pltpu.make_async_copy(summed.at[ctx], out_hbm.at[ctx, head], sem.at[head]).start()
         return carry
 
     lax.fori_loop(0, n_ctx, one, 0)
+    for head in range(n_head):
+        pltpu.make_async_copy(summed, out_hbm.at[:, head], sem.at[head]).wait()
 
 
 def shape_of(shape, dtype):
     return jax.ShapeDtypeStruct(shape, dtype)
 
 
-def call(body, name, scalars, arrays, out_shape, scratch, flops, space=VMEM):
+def call(body, name, specs, out_shape, scratch, flops, space=VMEM, limit=VMEM_LIMIT, aliases=()):
     return pl.pallas_call(
         body,
-        in_specs=[SMEM] * scalars + [space] * arrays,
-        out_specs=(space,) * len(out_shape),
+        in_specs=specs,
+        out_specs=space if isinstance(space, list) else [space] * len(out_shape),
         out_shape=out_shape,
         scratch_shapes=scratch,
-        compiler_params=pltpu.CompilerParams(vmem_limit_bytes=VMEM_LIMIT),
+        compiler_params=pltpu.CompilerParams(vmem_limit_bytes=limit),
         cost_estimate=pl.CostEstimate(
             flops=flops, bytes_accessed=1 << 22, transcendentals=0
         ),
+        input_output_aliases=dict(aliases),
         name=name,
     )
+
+
+def stats_shape(row_total):
+    return shape_of((STATS_SIZE // row_total, row_total), F32)
 
 
 def past_call(window, heads, pieces_shape, row_total, work):
@@ -511,9 +549,12 @@
     return call(
         functools.partial(past_kernel, window, heads),
         "past",
-        3,
-        4,
-        (shape_of((8, row_total), F32), shape_of(pieces_shape, BF16)),
+        [HBM] * 3 + [ANY, HBM],
+        (
+            stats_shape(row_total),
+            shape_of(pieces_shape, BF16),
+            shape_of(pieces_shape, BF16),
+        ),
         [
             rows,
             rows,
@@ -527,9 +568,12 @@
             dma((2, window)),
             dma((2,)),
             dma((2, window)),
+            dma((2, window)),
         ],
         4 * window * work,
         HBM,
+        PAST_LIMIT,
+        ((4, 2),),
     )
 
 
@@ -542,8 +586,7 @@
     return call(
         functools.partial(late_kernel, window, heads),
         "late",
-        3,
-        7,
+        [HBM] * 7,
         (shape_of((row_total, width), BF16), shape_of((row_total, width), BF16)),
         [
             rows,
@@ -570,11 +613,11 @@
     return call(
         functools.partial(own_forward_kernel, heads),
         "own_forward",
-        3,
-        4,
-        (shape_of((8, row_total), F32),) + tuple(shape_of((end, ROW_BLOCK), BF16) for end in ends),
-        [],
+        [SMEM] * 3 + [VMEM] * 4,
+        (stats_shape(row_total),) + tuple(shape_of((end, ROW_BLOCK), BF16) for end in ends),
+        [pltpu.VMEM((8, row_total), F32), pltpu.SemaphoreType.DMA((1,))],
         2 * work,
+        [HBM] + [VMEM] * len(ends),
     )
 
 
@@ -582,25 +625,29 @@
     return call(
         functools.partial(own_grads_kernel, heads),
         "own_grads",
-        0,
-        5 + row_total // ROW_BLOCK,
+        [VMEM] * 2 + [HBM] + [VMEM] * (2 + row_total // ROW_BLOCK),
         (
             shape_of((width, row_total), BF16),
             shape_of((width, row_total), BF16),
             shape_of((2, tile_rows, width), BF16),
         ),
-        [pltpu.VMEM((tile_rows, width), F32), pltpu.VMEM((tile_rows, width), F32)],
+        [
+            pltpu.VMEM((8, row_total), F32),
+            pltpu.SemaphoreType.DMA((1,)),
+            pltpu.VMEM((tile_rows, width), F32),
+            pltpu.VMEM((tile_rows, width), F32),
+        ],
         4 * work,
     )
 
 
-def small_call(body, name, out_shape, n_ctx, ordered=0):
+def small_call(body, name, scalars, specs, out_shape, scratch):
     return pl.pallas_call(
         body,
-        in_specs=[SMEM, SMEM, VMEM] + [HBM] * ordered,
-        out_specs=VMEM,
+        in_specs=[SMEM] * scalars + specs,
+        out_specs=HBM,
         out_shape=out_shape,
-        scratch_shapes=[pltpu.SMEM((n_ctx,), jnp.int32)],
+        scratch_shapes=scratch,
         compiler_params=pltpu.CompilerParams(vmem_limit_bytes=SMALL_LIMIT),
         name=name,
     )
@@ -626,16 +673,22 @@
     work = 2 * row_total * tile_rows * width
     fine = piece % 16 == 0
 
-    pieces = jnp.stack(
-        [tile.reshape(group, n_head, piece, width) for tile in (keys, values)], axis=2
-    )
-    mine = lax.dynamic_index_in_dim(pieces, y, 1, keepdims=False)
-    held = lax.all_to_all(jnp.concatenate([mine, mine]), "ctx", 0, 0, tiled=True)
+    shape = (2, group, 1, piece, width)
+    mine = [
+        lax.dynamic_index_in_dim(tile.reshape(group, n_head, piece, width), y, 1)
+        for tile in (keys, values)
+    ]
+    mine = jnp.concatenate([jnp.broadcast_to(part[None], shape) for part in mine], axis=2)
+    held = lax.all_to_all(
+        mine.reshape(n_ctx, 2, piece, width), "ctx", 0, 0, tiled=True
+    )
     packed = small_call(
         functools.partial(route_kernel, window),
         "route",
+        2,
+        [ANY],
         shape_of((group, n_head, window, 2, piece, width), BF16),
-        n_ctx,
+        [pltpu.SMEM((n_ctx,), jnp.int32), pltpu.SemaphoreType.DMA((group,))],
     )(place, tile_of, held)
     past = lax.all_to_all(
         packed.reshape(n_owners, window, 2, piece, width),
@@ -653,8 +706,8 @@
     own_stats, *own_weights = own_forward_call(heads, tile_rows, width, row_total, work)(
         *scalars, q_rows, g_rows, keys, values
     )
-    stats, terms = past_call(window, heads, pieces_shape, row_total, work)(
-        *scalars, q_rows, g_rows, own_stats, past
+    stats, terms, kept = past_call(window, heads, pieces_shape, row_total, work)(
+        q_rows, g_rows, own_stats, past, packed.reshape(pieces_shape)
     )
     own_out, own_dq, own_grads = own_grads_call(heads, tile_rows, width, row_total, work)(
         q_rows, g_rows, stats, keys, values, *own_weights
@@ -663,17 +716,23 @@
     if not fine:
         terms = terms.reshape(window, 2, n_owners, piece, width).transpose(2, 0, 1, 3, 4)
     terms = lax.all_to_all(terms, both, 0, 0, tiled=True, axis_index_groups=halves)
+    terms, own_grads = lax.optimization_barrier((terms, own_grads))
     summed = small_call(
         functools.partial(sum_kernel, window, group),
         "sum_terms",
+        2,
+        [VMEM],
         shape_of((n_ctx, n_head, 2, piece, width), BF16),
-        n_ctx,
-        1,
-    )(place, tile_of, terms.reshape(group, n_head, window, 2, piece, width), own_grads)
+        [
+            pltpu.SMEM((n_ctx,), jnp.int32),
+            pltpu.VMEM((n_ctx, 2, piece, width), BF16),
+            pltpu.SemaphoreType.DMA((n_head,)),
+        ],
+    )(place, tile_of, terms.reshape(group, n_head, window, 2, piece, width))
     summed = summed.reshape(n_ctx * n_head, 2, piece, width)
     far = lax.all_to_all(summed, both, 0, 0, tiled=True)
     attended, query_grad = late_call(window, heads, pieces_shape, row_total, work)(
-        *scalars, q_rows, g_rows, stats, past, own_out, own_dq, summed
+        q_rows, g_rows, stats, kept, own_out, own_dq, summed
     )
 
     if n_head == 2:

time: 83.9 us -> 81.5 us (0.971); the launches traced: 83.6 us -> 80.3 us
  Pallas kernels: 29 us -> 30.9 us
  waiting for transfers between devices: 23.4 us -> 21.6 us
  starting transfers between devices: 25.3 us -> 23.6 us
  other arithmetic: 2.72 us -> 1.84 us
    unnamed x10 -> x6, local copies, waits for them, and re-layouts: 2.41 us -> 0.67 us
    all_to_all x1, waiting for transfers between devices: 4.12 us -> 2.69 us  [on_device(): lax.all_to_all(packed.reshape(n_owners, window, 2, piece, width), both, 0...]
    pallas_call x1, Pallas kernels: 5.44 us -> 6.86 us  [on_device(): own_forward_call(heads, tile_rows, width, row_total, work)]
    all_to_all x1, starting transfers between devices: 7.67 us -> 6.26 us  [on_device(): lax.all_to_all(terms, both, 0, 0, tiled=True, axis_index_groups=halves)]
    broadcast_in_dim x0 -> x3, local copies, waits for them, and re-layouts: none -> 0.93 us  [on_device(): jnp.broadcast_to(part[None], shape)]
    squeeze x1 -> x0, other arithmetic: 0.89 us -> none  [on_device(): mine = lax.dynamic_index_in_dim(pieces, y, 1, keepdims=False)]
    all_to_all x1, waiting for transfers between devices: 3.22 us -> 2.34 us  [on_device(): lax.all_to_all(terms, both, 0, 0, tiled=True, axis_index_groups=halves)]
    pallas_call x1, Pallas kernels: 6.76 us -> 7.63 us  [on_device(): own_grads_call(heads, tile_rows, width, row_total, work)]
  transfers between devices with their start and end apart: 5 -> 5, of which waited for: 5 -> 5; matrix products, arithmetic and copies ran while one was open for 0% -> 0% of each run, Pallas kernels for 23% -> 26%
where the time goes in v1:
time: 81.5 us; the launch traced here: 80.3 us
  Pallas kernels  30.9 us (38%)
  starting transfers between devices  23.6 us (29%)
  waiting for transfers between devices  21.6 us (27%)
  other arithmetic  1.84 us (2%)
  local copies, waits for them, and re-layouts  1.63 us (2%)
    all_to_all x1, waiting for transfers between devices, on_device(): lax.all_to_all(mine.reshape(n_ctx, 2, piece, width), 'ctx', 0, 0, tiled=T...  10 us
    pallas_call x1, Pallas kernels, on_device(): own_grads_call(heads, tile_rows, width, row_total, work)  7.63 us
    all_to_all x1, starting transfers between devices, on_device(): lax.all_to_all(mine.reshape(n_ctx, 2, piece, width), 'ctx', 0, 0, tiled=T...  7.36 us
    pallas_call x1, Pallas kernels, on_device(): own_forward_call(heads, tile_rows, width, row_total, work)  6.86 us
    pallas_call x1, Pallas kernels, on_device(): late_call(window, heads, pieces_shape, row_total, work)  6.65 us
    pallas_call x1, Pallas kernels, on_device(): past_call(window, heads, pieces_shape, row_total, work)  6.6 us
    all_to_all x1, starting transfers between devices, on_device(): lax.all_to_all(terms, both, 0, 0, tiled=True, axis_index_groups=halves)  6.26 us
    ppermute x1, waiting for transfers between devices, on_device(): peer = lax.ppermute(own_grads, 'head', [(0, 1), (1, 0)])  4.73 us
  transfers between devices with their start and end apart: 5, of which 5 were waited for; matrix products, arithmetic and copies ran while one was open for 0% of the time, Pallas kernels for 26%

profile of v1, /device:TPU:0, one launch (start us, length us, event | category | flops | bytes accessed | tf_op | source)
XLA Modules:
  0.0 80.3 jit_solution(17491759534085922906)
XLA Ops:
  0.6 0.9 %dynamic-slice_bitcast_fusion = (bf16[8,32,128]{2,1,0:T(8,128)(2,1)S(1)}, bf16[8,32,128]{2,1,0:T(8,128)(2,1)S(1)}) fusion(bf16[8,2,32,128]{3,2,1,0:T(8,128)(2,1)} %bitcast.37, s32[]{:T(128)S(6)} %select_n.5, bf16[8,2,32,128]{3,2,1,0:T(8,128)(2,1)} %bitcast.36), kind=kLoop, calls=%fused_computation.7 | loop fusion | bytes 262148 | tf_op jit(solution)/shard_map/broadcast_in_dim | solution.py:681
  1.6 0.7 pad_maximum_fusion
  2.3 7.4 %all-to-all-start = ((bf16[16,2,32,128]{3,2,1,0:T(8,128)(2,1)}), bf16[16,2,32,128]{3,2,1,0:T(8,128)(2,1)S(1)}, u32[]{:S(2)}, u32[]{:S(2)}) async-start(bf16[16,2,32,128]{3,2,1,0:T(8,128)(2,1)} %bitcast.7), calls=%async_computation | async-start | bytes 524288 | tf_op jit(solution)/shard_map/all_to_all | solution.py:682
  9.7 10.0 %all-to-all-done.held_hbm = bf16[16,2,32,128]{3,2,1,0:T(8,128)(2,1)S(1)} async-done(((bf16[16,2,32,128]{3,2,1,0:T(8,128)(2,1)}), bf16[16,2,32,128]{3,2,1,0:T(8,128)(2,1)S(1)}, u32[]{:S(2)}, u32[]{:S(2)}) %all-to-all-start) | async-done | bytes 262176 | tf_op jit(solution)/shard_map/all_to_all | solution.py:682
  19.7 0.0 copy-start
  19.7 0.7 copy-done
  20.4 1.5 %route.1 = bf16[8,2,2,2,32,128]{5,4,3,2,1,0:T(8,128)(2,1)} custom-call(s32[1]{0:T(128)} %bitcast.2.place_ref, s32[16]{0:T(128)S(1)} %copy-done, bf16[16,2,32,128]{3,2,1,0:T(8,128)(2,1)S(1)} %all-to-all-done.held_hbm), custom_call_target="tpu_custom_call" | custom-call | tf_op jit(solution)/shard_map/route/pallas_call | solution.py:685
  21.8 3.6 %all-to-all-start.1 = ((bf16[16,2,2,32,128]{4,3,2,1,0:T(8,128)(2,1)}), bf16[16,2,2,32,128]{4,3,2,1,0:T(8,128)(2,1)S(1)}, u32[]{:S(2)}, u32[]{:S(2)}) async-start(bf16[16,2,2,32,128]{4,3,2,1,0:T(8,128)(2,1)} %bitcast.8.kept_in_hbm), calls=%async_computation.1 | async-start | bytes 1048576 | tf_op jit(solution)/shard_map/all_to_all | solution.py:693
  25.4 6.9 %own_forward.1 = (f32[1024,4096]{1,0:T(8,128)}, bf16[128,1024]{1,0:T(8,128)(2,1)}, bf16[256,1024]{1,0:T(8,128)(2,1)}, bf16[384,1024]{1,0:T(8,128)(2,1)}, bf16[512,1024]{1,0:T(8,128)(2,1)}) custom-call(s32[1]{0:T(128)} %bitcast.2.place_ref, s32[16]{0:T(128)} %lengths_ref.1, s32[16]{0:T(128)} %tile_of_ref.5, bf16[4096,128]{1,0:T(8,128)(2,1)} %bitcast.28, ...), custom_call_target="tpu_custom_call" | custom-call | flops 1073741824 | bytes 4194304 | tf_op jit(solution)/shard_map/own_forward/pallas_call | solution.py:706
  32.3 2.7 %all-to-all-done.1.past_hbm = bf16[16,2,2,32,128]{4,3,2,1,0:T(8,128)(2,1)S(1)} async-done(((bf16[16,2,2,32,128]{4,3,2,1,0:T(8,128)(2,1)}), bf16[16,2,2,32,128]{4,3,2,1,0:T(8,128)(2,1)S(1)}, u32[]{:S(2)}, u32[]{:S(2)}) %all-to-all-start.1) | async-done | bytes 524320 | tf_op jit(solution)/shard_map/all_to_all | solution.py:693
  35.0 0.0 copy-start.1
  35.0 6.6 %past.1 = (f32[1024,4096]{1,0:T(8,128)}, bf16[16,2,2,32,128]{4,3,2,1,0:T(8,128)(2,1)}, bf16[16,2,2,32,128]{4,3,2,1,0:T(8,128)(2,1)}) custom-call(bf16[4096,128]{1,0:T(8,128)(2,1)} %bitcast.29, bf16[4096,128]{1,0:T(8,128)(2,1)} %bitcast.33, f32[1024,4096]{1,0:T(8,128)} %get-tuple-element.22.own_stats_hbm, ...), custom_call_target="tpu_custom_call", output_to_operand_aliasing={{2}: (4, {})} | custom-call | flops 4294967296 | bytes 4194304 | tf_op jit(solution)/shard_map/past/pallas_call | solution.py:709
  41.6 6.3 %all-to-all-start.2 = ((bf16[16,2,2,32,128]{4,3,2,1,0:T(8,128)(2,1)}), bf16[16,2,2,32,128]{4,3,2,1,0:T(8,128)(2,1)S(1)}, u32[]{:S(2)}, u32[]{:S(2)}) async-start(bf16[16,2,2,32,128]{4,3,2,1,0:T(8,128)(2,1)} %get-tuple-element.23), calls=%async_computation.2 | async-start | bytes 1048576 | tf_op jit(solution)/shard_map/all_to_all | solution.py:718
  47.9 7.6 %own_grads.1 = (bf16[128,4096]{1,0:T(8,128)(2,1)}, bf16[128,4096]{1,0:T(8,128)(2,1)}, bf16[2,512,128]{2,1,0:T(8,128)(2,1)}) custom-call(bf16[4096,128]{1,0:T(8,128)(2,1)} %bitcast.30, bf16[4096,128]{1,0:T(8,128)(2,1)} %bitcast.34, f32[1024,4096]{1,0:T(8,128)} %get-tuple-element.24.stats_hbm, bf16[512,128]{1,0:T(8,128)(2,1)} %k_ref.3, ...), custom_call_target="tpu_custom_call" | custom-call | flops 2147483648 | bytes 4194304 | tf_op jit(solution)/shard_map/own_grads/pallas_call | solution.py:712
  55.5 0.0 copy-start.2
  55.5 2.3 %all-to-all-done.2 = bf16[16,2,2,32,128]{4,3,2,1,0:T(8,128)(2,1)S(1)} async-done(((bf16[16,2,2,32,128]{4,3,2,1,0:T(8,128)(2,1)}), bf16[16,2,2,32,128]{4,3,2,1,0:T(8,128)(2,1)S(1)}, u32[]{:S(2)}, u32[]{:S(2)}) %all-to-all-start.2) | async-done | bytes 524320 | tf_op jit(solution)/shard_map/all_to_all | solution.py:718
  57.9 0.0 copy-done.1
  57.9 1.7 %sum_terms.1 = bf16[16,2,2,32,128]{4,3,2,1,0:T(8,128)(2,1)} custom-call(s32[1]{0:T(128)} %bitcast.2.place_ref, s32[16]{0:T(128)S(1)} %copy-done.1, bf16[8,2,2,2,32,128]{5,4,3,2,1,0:T(8,128)(2,1)S(1)} %bitcast.27), custom_call_target="tpu_custom_call" | custom-call | tf_op jit(solution)/shard_map/sum_terms/pallas_call | solution.py:720
  59.6 4.6 %all-to-all-start.3 = ((bf16[32,2,32,128]{3,2,1,0:T(8,128)(2,1)}), bf16[32,2,32,128]{3,2,1,0:T(8,128)(2,1)S(1)}, u32[]{:S(2)}, u32[]{:S(2)}) async-start(bf16[32,2,32,128]{3,2,1,0:T(8,128)(2,1)} %bitcast.10.summed_hbm), calls=%async_computation.3 | async-start | bytes 1048576 | tf_op jit(solution)/shard_map/all_to_all | solution.py:733
  64.1 1.8 %collective-permute-start = (bf16[2,512,128]{2,1,0:T(8,128)(2,1)}, bf16[2,512,128]{2,1,0:T(8,128)(2,1)S(1)}, u32[]{:S(2)}, u32[]{:S(2)}) collective-permute-start(bf16[2,512,128]{2,1,0:T(8,128)(2,1)} %get-tuple-element.30), channel_id=1, source_target_pairs={{0,1},{1,0},{2,3},{3,2},{4,5},{5,4},{6,7},{7,6},{8,9},{9,8},{10,11... | collective-permute-start | bytes 786440 | tf_op jit(solution)/shard_map/ppermute | solution.py:739
  66.0 6.7 %late.1 = (bf16[4096,128]{1,0:T(8,128)(2,1)}, bf16[4096,128]{1,0:T(8,128)(2,1)}) custom-call(bf16[4096,128]{1,0:T(8,128)(2,1)} %bitcast.31, bf16[4096,128]{1,0:T(8,128)(2,1)} %bitcast.35, f32[1024,4096]{1,0:T(8,128)} %get-tuple-element.24.stats_hbm, bf16[16,2,2,32,128]{4,3,2,1,0:T(8,128)(2,1)} %get-tuple-element.32.past_hbm, ...), custom_call_target="tpu_custom_call" | custom-call | flops 4294967296 | bytes 4194304 | tf_op jit(solution)/shard_map/late/pallas_call | solution.py:734
  72.6 4.7 %collective-permute-done = bf16[2,512,128]{2,1,0:T(8,128)(2,1)S(1)} collective-permute-done((bf16[2,512,128]{2,1,0:T(8,128)(2,1)}, bf16[2,512,128]{2,1,0:T(8,128)(2,1)S(1)}, u32[]{:S(2)}, u32[]{:S(2)}) %collective-permute-start) | collective-permute-done | bytes 262176 | tf_op jit(solution)/shard_map/ppermute | solution.py:739
  77.4 1.8 %all-to-all-done.3 = bf16[32,2,32,128]{3,2,1,0:T(8,128)(2,1)S(1)} async-done(((bf16[32,2,32,128]{3,2,1,0:T(8,128)(2,1)}), bf16[32,2,32,128]{3,2,1,0:T(8,128)(2,1)S(1)}, u32[]{:S(2)}, u32[]{:S(2)}) %all-to-all-start.3) | async-done | bytes 524320 | tf_op jit(solution)/shard_map/all_to_all | solution.py:733
  79.1 0.0 copy-done.2
  79.1 0.1 convert_add_fusion
  79.2 0.1 convert_element_type.12
  79.3 0.1 slice_add_fusion
  79.5 0.8 %fusion = (f32[512,128]{1,0:T(8,128)}, f32[512,128]{1,0:T(8,128)}) fusion(f32[2,512,128]{2,1,0:T(8,128)S(1)} %convert_add_fusion, f32[16,1,32,128]{3,2,1,0:T(8,128)S(1)} %get-tuple-element.42, f32[16,1,32,128]{3,2,1,0:T(8,128)S(1)} %get-tuple-element.43), kind=kLoop, calls=%fused_computation.3 | loop fusion | flops 131072 | bytes 1572864 | tf_op jit(solution)/shard_map/add | solution.py:751
  (3 shorter events, 0.1 us)
Async XLA Ops:
  2.3 17.4 %all-to-all-start = ((bf16[16,2,32,128]{3,2,1,0:T(8,128)(2,1)}), bf16[16,2,32,128]{3,2,1,0:T(8,128)(2,1)S(1)}, u32[]{:S(2)}, u32[]{:S(2)}) async-start(bf16[16,2,32,128]{3,2,1,0:T(8,128)(2,1)} %bitcast.7), calls=%async_computation | async-start | bytes 524288 | tf_op jit(solution)/shard_map/all_to_all | solution.py:682
  19.7 0.7 copy-start
  21.8 13.2 %all-to-all-start.1 = ((bf16[16,2,2,32,128]{4,3,2,1,0:T(8,128)(2,1)}), bf16[16,2,2,32,128]{4,3,2,1,0:T(8,128)(2,1)S(1)}, u32[]{:S(2)}, u32[]{:S(2)}) async-start(bf16[16,2,2,32,128]{4,3,2,1,0:T(8,128)(2,1)} %bitcast.8.kept_in_hbm), calls=%async_computation.1 | async-start | bytes 1048576 | tf_op jit(solution)/shard_map/all_to_all | solution.py:693
  35.0 22.9 %copy-start.1 = (s32[16]{0:T(128)S(1)}, s32[16]{0:T(128)}, u32[]{:S(2)}) copy-start(s32[16]{0:T(128)} %tile_of_ref.5) | copy-start | bytes 196
  41.6 16.3 %all-to-all-start.2 = ((bf16[16,2,2,32,128]{4,3,2,1,0:T(8,128)(2,1)}), bf16[16,2,2,32,128]{4,3,2,1,0:T(8,128)(2,1)S(1)}, u32[]{:S(2)}, u32[]{:S(2)}) async-start(bf16[16,2,2,32,128]{4,3,2,1,0:T(8,128)(2,1)} %get-tuple-element.23), calls=%async_computation.2 | async-start | bytes 1048576 | tf_op jit(solution)/shard_map/all_to_all | solution.py:718
  55.5 23.6 %copy-start.2 = (bf16[2,512,128]{2,1,0:T(8,128)(2,1)S(1)}, bf16[2,512,128]{2,1,0:T(8,128)(2,1)}, u32[]{:S(2)}) copy-start(bf16[2,512,128]{2,1,0:T(8,128)(2,1)} %get-tuple-element.30) | copy-start | bytes 786436
  59.6 19.6 %all-to-all-start.3 = ((bf16[32,2,32,128]{3,2,1,0:T(8,128)(2,1)}), bf16[32,2,32,128]{3,2,1,0:T(8,128)(2,1)S(1)}, u32[]{:S(2)}, u32[]{:S(2)}) async-start(bf16[32,2,32,128]{3,2,1,0:T(8,128)(2,1)} %bitcast.10.summed_hbm), calls=%async_computation.3 | async-start | bytes 1048576 | tf_op jit(solution)/shard_map/all_to_all | solution.py:733
  64.1 13.2 %collective-permute-start = (bf16[2,512,128]{2,1,0:T(8,128)(2,1)}, bf16[2,512,128]{2,1,0:T(8,128)(2,1)S(1)}, u32[]{:S(2)}, u32[]{:S(2)}) collective-permute-start(bf16[2,512,128]{2,1,0:T(8,128)(2,1)} %get-tuple-element.30), channel_id=1, source_target_pairs={{0,1},{1,0},{2,3},{3,2},{4,5},{5,4},{6,7},{7,6},{8,9},{9,8},{10,11... | collective-permute-start | bytes 786440 | tf_op jit(solution)/shard_map/ppermute | solution.py:739

commit v2 on v1

--- a/solution.py
+++ b/solution.py
@@ -262,16 +262,17 @@
     stats_in = pltpu.make_async_copy(own_stats_hbm.at[0:8], own_stats_ref, stats_sem.at[0])
     stats_out = pltpu.make_async_copy(stats_ref, stats_hbm.at[0:8], stats_sem.at[1])
 
+    stats_in.start()
     start_all(past.copies(0, past_sem))
     start_all(chunk_copies(pairs, in_sem, 0))
-    stats_in.start()
     start_all(past.copies(1, past_sem))
     for chunk in range(1, chunks):
         start_all(chunk_copies(pairs, in_sem, chunk))
     dk_acc[...] = jnp.zeros_like(dk_acc)
     dv_acc[...] = jnp.zeros_like(dv_acc)
-    wait_all(past.copies(0, past_sem) + past.copies(1, past_sem) + [stats_in])
+    stats_in.wait()
     past.plan(own_stats_ref)
+    wait_all(past.copies(0, past_sem) + past.copies(1, past_sem))
     stats_ref[3:6, :] = own_stats_ref[3:6, :]
     keep = [
         pltpu.make_async_copy(
@@ -492,7 +493,7 @@
     holders(tile_of_ref, holder)
     first = lax.div(place_ref[0], group) * group
 
-    def one(ctx, carry):
+    for ctx in range(n_ctx):
         total = jnp.zeros(summed.shape[1:], F32)
         for slot in range(window):
             tile = tile_of_ref[ctx] + (window - slot)
@@ -506,9 +507,6 @@
         summed[ctx] = total.astype(BF16)
         for head in range(n_head):
             pltpu.make_async_copy(summed.at[ctx], out_hbm.at[ctx, head], sem.at[head]).start()
-        return carry
-
-    lax.fori_loop(0, n_ctx, one, 0)
     for head in range(n_head):
         pltpu.make_async_copy(summed, out_hbm.at[:, head], sem.at[head]).wait()
 

time: 81.5 us -> 80.6 us (0.989)
  Pallas kernels: 30.9 us -> 29.8 us
    all_to_all x1, starting transfers between devices: 6.26 us -> 8.11 us  [on_device(): lax.all_to_all(terms, both, 0, 0, tiled=True, axis_index_groups=halves)]
    all_to_all x1, starting transfers between devices: 4.58 us -> 2.99 us  [on_device(): far = lax.all_to_all(summed, both, 0, 0, tiled=True)]
  transfers between devices with their start and end apart: 5 -> 5, of which waited for: 5 -> 5; matrix products, arithmetic and copies ran while one was open for 0% -> 0% of each run, Pallas kernels for 26% -> 27%
where the time goes in v2:
time: 80.6 us; the launch traced here: 79.5 us
  Pallas kernels  29.8 us (37%)
  starting transfers between devices  23.9 us (30%)
  waiting for transfers between devices  21.6 us (27%)
  other arithmetic  1.84 us (2%)
  local copies, waits for them, and re-layouts  1.63 us (2%)
    all_to_all x1, waiting for transfers between devices, on_device(): lax.all_to_all(mine.reshape(n_ctx, 2, piece, width), 'ctx', 0, 0, tiled=T...  10 us
    all_to_all x1, starting transfers between devices, on_device(): lax.all_to_all(terms, both, 0, 0, tiled=True, axis_index_groups=halves)  8.11 us
    pallas_call x1, Pallas kernels, on_device(): own_grads_call(heads, tile_rows, width, row_total, work)  7.63 us
    all_to_all x1, starting transfers between devices, on_device(): lax.all_to_all(mine.reshape(n_ctx, 2, piece, width), 'ctx', 0, 0, tiled=T...  7.36 us
    pallas_call x1, Pallas kernels, on_device(): own_forward_call(heads, tile_rows, width, row_total, work)  6.86 us
    pallas_call x1, Pallas kernels, on_device(): late_call(window, heads, pieces_shape, row_total, work)  6.59 us
    pallas_call x1, Pallas kernels, on_device(): past_call(window, heads, pieces_shape, row_total, work)  5.83 us
    ppermute x1, waiting for transfers between devices, on_device(): peer = lax.ppermute(own_grads, 'head', [(0, 1), (1, 0)])  4.79 us
  transfers between devices with their start and end apart: 5, of which 5 were waited for; matrix products, arithmetic and copies ran while one was open for 0% of the time, Pallas kernels for 27%

profile of v2, /device:TPU:0, one launch (start us, length us, event | category | flops | bytes accessed | tf_op | source)
XLA Modules:
  0.0 79.5 jit_solution(11349094678809917155)
XLA Ops:
  0.6 0.9 %dynamic-slice_bitcast_fusion = (bf16[8,32,128]{2,1,0:T(8,128)(2,1)S(1)}, bf16[8,32,128]{2,1,0:T(8,128)(2,1)S(1)}) fusion(bf16[8,2,32,128]{3,2,1,0:T(8,128)(2,1)} %bitcast.37, s32[]{:T(128)S(6)} %select_n.5, bf16[8,2,32,128]{3,2,1,0:T(8,128)(2,1)} %bitcast.36), kind=kLoop, calls=%fused_computation.7 | loop fusion | bytes 262148 | tf_op jit(solution)/shard_map/broadcast_in_dim | solution.py:679
  1.6 0.7 pad_maximum_fusion
  2.3 7.4 %all-to-all-start = ((bf16[16,2,32,128]{3,2,1,0:T(8,128)(2,1)}), bf16[16,2,32,128]{3,2,1,0:T(8,128)(2,1)S(1)}, u32[]{:S(2)}, u32[]{:S(2)}) async-start(bf16[16,2,32,128]{3,2,1,0:T(8,128)(2,1)} %bitcast.7), calls=%async_computation | async-start | bytes 524288 | tf_op jit(solution)/shard_map/all_to_all | solution.py:680
  9.7 10.0 %all-to-all-done.held_hbm = bf16[16,2,32,128]{3,2,1,0:T(8,128)(2,1)S(1)} async-done(((bf16[16,2,32,128]{3,2,1,0:T(8,128)(2,1)}), bf16[16,2,32,128]{3,2,1,0:T(8,128)(2,1)S(1)}, u32[]{:S(2)}, u32[]{:S(2)}) %all-to-all-start) | async-done | bytes 262176 | tf_op jit(solution)/shard_map/all_to_all | solution.py:680
  19.7 0.0 copy-start
  19.7 0.7 copy-done
  20.4 1.5 %route.1 = bf16[8,2,2,2,32,128]{5,4,3,2,1,0:T(8,128)(2,1)} custom-call(s32[1]{0:T(128)} %bitcast.2.place_ref, s32[16]{0:T(128)S(1)} %copy-done, bf16[16,2,32,128]{3,2,1,0:T(8,128)(2,1)S(1)} %all-to-all-done.held_hbm), custom_call_target="tpu_custom_call" | custom-call | tf_op jit(solution)/shard_map/route/pallas_call | solution.py:683
  21.8 3.6 %all-to-all-start.1 = ((bf16[16,2,2,32,128]{4,3,2,1,0:T(8,128)(2,1)}), bf16[16,2,2,32,128]{4,3,2,1,0:T(8,128)(2,1)S(1)}, u32[]{:S(2)}, u32[]{:S(2)}) async-start(bf16[16,2,2,32,128]{4,3,2,1,0:T(8,128)(2,1)} %bitcast.8.kept_in_hbm), calls=%async_computation.1 | async-start | bytes 1048576 | tf_op jit(solution)/shard_map/all_to_all | solution.py:691
  25.4 6.9 %own_forward.1 = (f32[1024,4096]{1,0:T(8,128)}, bf16[128,1024]{1,0:T(8,128)(2,1)}, bf16[256,1024]{1,0:T(8,128)(2,1)}, bf16[384,1024]{1,0:T(8,128)(2,1)}, bf16[512,1024]{1,0:T(8,128)(2,1)}) custom-call(s32[1]{0:T(128)} %bitcast.2.place_ref, s32[16]{0:T(128)} %lengths_ref.1, s32[16]{0:T(128)} %tile_of_ref.5, bf16[4096,128]{1,0:T(8,128)(2,1)} %bitcast.28, ...), custom_call_target="tpu_custom_call" | custom-call | flops 1073741824 | bytes 4194304 | tf_op jit(solution)/shard_map/own_forward/pallas_call | solution.py:704
  32.3 2.7 %all-to-all-done.1.past_hbm = bf16[16,2,2,32,128]{4,3,2,1,0:T(8,128)(2,1)S(1)} async-done(((bf16[16,2,2,32,128]{4,3,2,1,0:T(8,128)(2,1)}), bf16[16,2,2,32,128]{4,3,2,1,0:T(8,128)(2,1)S(1)}, u32[]{:S(2)}, u32[]{:S(2)}) %all-to-all-start.1) | async-done | bytes 524320 | tf_op jit(solution)/shard_map/all_to_all | solution.py:691
  35.0 0.0 copy-start.1
  35.0 5.8 %past.1 = (f32[1024,4096]{1,0:T(8,128)}, bf16[16,2,2,32,128]{4,3,2,1,0:T(8,128)(2,1)}, bf16[16,2,2,32,128]{4,3,2,1,0:T(8,128)(2,1)}) custom-call(bf16[4096,128]{1,0:T(8,128)(2,1)} %bitcast.29, bf16[4096,128]{1,0:T(8,128)(2,1)} %bitcast.33, f32[1024,4096]{1,0:T(8,128)} %get-tuple-element.22.own_stats_hbm, ...), custom_call_target="tpu_custom_call", output_to_operand_aliasing={{2}: (4, {})} | custom-call | flops 4294967296 | bytes 4194304 | tf_op jit(solution)/shard_map/past/pallas_call | solution.py:707
  40.8 8.1 %all-to-all-start.2 = ((bf16[16,2,2,32,128]{4,3,2,1,0:T(8,128)(2,1)}), bf16[16,2,2,32,128]{4,3,2,1,0:T(8,128)(2,1)S(1)}, u32[]{:S(2)}, u32[]{:S(2)}) async-start(bf16[16,2,2,32,128]{4,3,2,1,0:T(8,128)(2,1)} %get-tuple-element.23), calls=%async_computation.2 | async-start | bytes 1048576 | tf_op jit(solution)/shard_map/all_to_all | solution.py:716
  49.0 7.6 %own_grads.1 = (bf16[128,4096]{1,0:T(8,128)(2,1)}, bf16[128,4096]{1,0:T(8,128)(2,1)}, bf16[2,512,128]{2,1,0:T(8,128)(2,1)}) custom-call(bf16[4096,128]{1,0:T(8,128)(2,1)} %bitcast.30, bf16[4096,128]{1,0:T(8,128)(2,1)} %bitcast.34, f32[1024,4096]{1,0:T(8,128)} %get-tuple-element.24.stats_hbm, bf16[512,128]{1,0:T(8,128)(2,1)} %k_ref.3, ...), custom_call_target="tpu_custom_call" | custom-call | flops 2147483648 | bytes 4194304 | tf_op jit(solution)/shard_map/own_grads/pallas_call | solution.py:710
  56.6 0.0 copy-start.2
  56.6 2.3 %all-to-all-done.2 = bf16[16,2,2,32,128]{4,3,2,1,0:T(8,128)(2,1)S(1)} async-done(((bf16[16,2,2,32,128]{4,3,2,1,0:T(8,128)(2,1)}), bf16[16,2,2,32,128]{4,3,2,1,0:T(8,128)(2,1)S(1)}, u32[]{:S(2)}, u32[]{:S(2)}) %all-to-all-start.2) | async-done | bytes 524320 | tf_op jit(solution)/shard_map/all_to_all | solution.py:716
  58.9 0.0 copy-done.1
  58.9 1.4 %sum_terms.1 = bf16[16,2,2,32,128]{4,3,2,1,0:T(8,128)(2,1)} custom-call(s32[1]{0:T(128)} %bitcast.2.place_ref, s32[16]{0:T(128)S(1)} %copy-done.1, bf16[8,2,2,2,32,128]{5,4,3,2,1,0:T(8,128)(2,1)S(1)} %bitcast.27), custom_call_target="tpu_custom_call" | custom-call | tf_op jit(solution)/shard_map/sum_terms/pallas_call | solution.py:718
  60.4 3.0 %all-to-all-start.3 = ((bf16[32,2,32,128]{3,2,1,0:T(8,128)(2,1)}), bf16[32,2,32,128]{3,2,1,0:T(8,128)(2,1)S(1)}, u32[]{:S(2)}, u32[]{:S(2)}) async-start(bf16[32,2,32,128]{3,2,1,0:T(8,128)(2,1)} %bitcast.10.summed_hbm), calls=%async_computation.3 | async-start | bytes 1048576 | tf_op jit(solution)/shard_map/all_to_all | solution.py:731
  63.4 1.8 %collective-permute-start = (bf16[2,512,128]{2,1,0:T(8,128)(2,1)}, bf16[2,512,128]{2,1,0:T(8,128)(2,1)S(1)}, u32[]{:S(2)}, u32[]{:S(2)}) collective-permute-start(bf16[2,512,128]{2,1,0:T(8,128)(2,1)} %get-tuple-element.30), channel_id=1, source_target_pairs={{0,1},{1,0},{2,3},{3,2},{4,5},{5,4},{6,7},{7,6},{8,9},{9,8},{10,11... | collective-permute-start | bytes 786440 | tf_op jit(solution)/shard_map/ppermute | solution.py:737
  65.2 6.6 %late.1 = (bf16[4096,128]{1,0:T(8,128)(2,1)}, bf16[4096,128]{1,0:T(8,128)(2,1)}) custom-call(bf16[4096,128]{1,0:T(8,128)(2,1)} %bitcast.31, bf16[4096,128]{1,0:T(8,128)(2,1)} %bitcast.35, f32[1024,4096]{1,0:T(8,128)} %get-tuple-element.24.stats_hbm, bf16[16,2,2,32,128]{4,3,2,1,0:T(8,128)(2,1)} %get-tuple-element.32.past_hbm, ...), custom_call_target="tpu_custom_call" | custom-call | flops 4294967296 | bytes 4194304 | tf_op jit(solution)/shard_map/late/pallas_call | solution.py:732
  71.8 4.8 %collective-permute-done = bf16[2,512,128]{2,1,0:T(8,128)(2,1)S(1)} collective-permute-done((bf16[2,512,128]{2,1,0:T(8,128)(2,1)}, bf16[2,512,128]{2,1,0:T(8,128)(2,1)S(1)}, u32[]{:S(2)}, u32[]{:S(2)}) %collective-permute-start) | collective-permute-done | bytes 262176 | tf_op jit(solution)/shard_map/ppermute | solution.py:737
  76.6 1.8 %all-to-all-done.3 = bf16[32,2,32,128]{3,2,1,0:T(8,128)(2,1)S(1)} async-done(((bf16[32,2,32,128]{3,2,1,0:T(8,128)(2,1)}), bf16[32,2,32,128]{3,2,1,0:T(8,128)(2,1)S(1)}, u32[]{:S(2)}, u32[]{:S(2)}) %all-to-all-start.3) | async-done | bytes 524320 | tf_op jit(solution)/shard_map/all_to_all | solution.py:731
  78.4 0.0 copy-done.2
  78.4 0.1 convert_add_fusion
  78.4 0.1 convert_element_type.12
  78.6 0.1 slice_add_fusion
  78.7 0.8 %fusion = (f32[512,128]{1,0:T(8,128)}, f32[512,128]{1,0:T(8,128)}) fusion(f32[2,512,128]{2,1,0:T(8,128)S(1)} %convert_add_fusion, f32[16,1,32,128]{3,2,1,0:T(8,128)S(1)} %get-tuple-element.42, f32[16,1,32,128]{3,2,1,0:T(8,128)S(1)} %get-tuple-element.43), kind=kLoop, calls=%fused_computation.3 | loop fusion | flops 131072 | bytes 1572864 | tf_op jit(solution)/shard_map/add | solution.py:749
  (3 shorter events, 0.1 us)
Async XLA Ops:
  2.3 17.4 %all-to-all-start = ((bf16[16,2,32,128]{3,2,1,0:T(8,128)(2,1)}), bf16[16,2,32,128]{3,2,1,0:T(8,128)(2,1)S(1)}, u32[]{:S(2)}, u32[]{:S(2)}) async-start(bf16[16,2,32,128]{3,2,1,0:T(8,128)(2,1)} %bitcast.7), calls=%async_computation | async-start | bytes 524288 | tf_op jit(solution)/shard_map/all_to_all | solution.py:680
  19.7 0.7 copy-start
  21.8 13.2 %all-to-all-start.1 = ((bf16[16,2,2,32,128]{4,3,2,1,0:T(8,128)(2,1)}), bf16[16,2,2,32,128]{4,3,2,1,0:T(8,128)(2,1)S(1)}, u32[]{:S(2)}, u32[]{:S(2)}) async-start(bf16[16,2,2,32,128]{4,3,2,1,0:T(8,128)(2,1)} %bitcast.8.kept_in_hbm), calls=%async_computation.1 | async-start | bytes 1048576 | tf_op jit(solution)/shard_map/all_to_all | solution.py:691
  35.0 23.9 %copy-start.1 = (s32[16]{0:T(128)S(1)}, s32[16]{0:T(128)}, u32[]{:S(2)}) copy-start(s32[16]{0:T(128)} %tile_of_ref.5) | copy-start | bytes 196
  40.8 18.1 %all-to-all-start.2 = ((bf16[16,2,2,32,128]{4,3,2,1,0:T(8,128)(2,1)}), bf16[16,2,2,32,128]{4,3,2,1,0:T(8,128)(2,1)S(1)}, u32[]{:S(2)}, u32[]{:S(2)}) async-start(bf16[16,2,2,32,128]{4,3,2,1,0:T(8,128)(2,1)} %get-tuple-element.23), calls=%async_computation.2 | async-start | bytes 1048576 | tf_op jit(solution)/shard_map/all_to_all | solution.py:716
  56.6 21.8 %copy-start.2 = (bf16[2,512,128]{2,1,0:T(8,128)(2,1)S(1)}, bf16[2,512,128]{2,1,0:T(8,128)(2,1)}, u32[]{:S(2)}) copy-start(bf16[2,512,128]{2,1,0:T(8,128)(2,1)} %get-tuple-element.30) | copy-start | bytes 786436
  60.4 18.0 %all-to-all-start.3 = ((bf16[32,2,32,128]{3,2,1,0:T(8,128)(2,1)}), bf16[32,2,32,128]{3,2,1,0:T(8,128)(2,1)S(1)}, u32[]{:S(2)}, u32[]{:S(2)}) async-start(bf16[32,2,32,128]{3,2,1,0:T(8,128)(2,1)} %bitcast.10.summed_hbm), calls=%async_computation.3 | async-start | bytes 1048576 | tf_op jit(solution)/shard_map/all_to_all | solution.py:731
  63.4 13.2 %collective-permute-start = (bf16[2,512,128]{2,1,0:T(8,128)(2,1)}, bf16[2,512,128]{2,1,0:T(8,128)(2,1)S(1)}, u32[]{:S(2)}, u32[]{:S(2)}) collective-permute-start(bf16[2,512,128]{2,1,0:T(8,128)(2,1)} %get-tuple-element.30), channel_id=1, source_target_pairs={{0,1},{1,0},{2,3},{3,2},{4,5},{5,4},{6,7},{7,6},{8,9},{9,8},{10,11... | collective-permute-start | bytes 786440 | tf_op jit(solution)/shard_map/ppermute | solution.py:737
